TPU v7x, 128 devices: a whole 4x4x4 slice. The times are simulated.
128 devices in a mesh: row: 16 (over y, x_hi, core), col: 8 (over x_lo, z).
Axes of the slice: x: 4 (x_hi: 2, x_lo: 2; x = x_hi * 2 + x_lo), y: 4, z: 4, core: 2. Of those that a mesh axis runs over, the one named last changes fastest.
Arguments:
- object_field: float32 [2, 8192, 4096], P(None, 'row', 'col'), may hold values from -6 to 6
- probe: float32 [2, 4, 256, 256], replicated, may hold values from -5 to 5
- amplitudes: float32 [16, 8, 6, 256, 256], P('row', 'col'), may hold values from 0.1 to 2
- positions: int32 [16, 8, 6, 2], P('row', 'col'), may hold values from 1 to 511, as said below
- counts: int32 [16, 8], P('row', 'col'), may hold values from 1 to 6, as said below
Outputs:
- object_new: float32 [2, 8192, 4096], P(None, 'row', 'col')
- probe_new: float32 [2, 4, 256, 256], replicated
- position_grad: float32 [16, 8, 6, 2], P('row', 'col')
Inputs may be any that keep to these rules, and one draw needn't show every extreme that they name: `counts`: live scan positions of each tile; slots at or past the count are unused and ignored; some tile has all 6 slots live. `positions`: offset of a patch's first cell in its tile extended by 128 cells on each side.
All inputs are finite; a program needn't handle non-finite values.
Results may differ from a plain program's by a relative error of at most 0.0003.
Values sent between devices are 32-bit elements; how exact they have to be, the bound alone decides.
A program may use at most 192 MiB of HBM per device.

v0:
```python
import math

import ml_dtypes
import numpy as np
import jax
import jax.numpy as jnp
from jax import lax
from jax.experimental import pallas as pl
from jax.experimental.pallas import tpu as pltpu
from jax.sharding import PartitionSpec as P

HALO = 128
INTENSITY_FLOOR = 0.1
EPSILON = 1e-06
F32 = jnp.float32
BF16 = jnp.bfloat16


def padded(x, sides, width):
    for axis, dim in sides:
        peers, length = (lax.axis_size(axis), x.shape[dim])
        up = [(i, (i + 1) % peers) for i in range(peers - 1)]
        down = [(j, i) for i, j in up]
        last = lax.slice_in_dim(x, length - width, length, axis=dim)
        first = lax.slice_in_dim(x, 0, width, axis=dim)
        before = lax.ppermute(last, axis, up)
        after = lax.ppermute(first, axis, down)
        x = jnp.concatenate([before, x, after], axis=dim)
    return x


def shifted(x, axis, by):
    peers = lax.axis_size(axis)
    pairs = [(i, i + by) for i in range(peers) if 0 <= i + by < peers]
    return lax.ppermute(x, axis, pairs)


def dft_tables(pixels):
    half = pixels // 2
    k = np.arange(half)[:, None]
    n = np.arange(half)[None, :]
    out = []
    for parity in (0, 1):
        angle = (n * (2 * k + parity) % pixels) * (2.0 * math.pi / pixels)
        c = np.cos(angle) / math.sqrt(pixels)
        s = np.sin(angle) / math.sqrt(pixels)
        out.append(np.block([[c, s], [-s, c]]))
    both = []
    for m in (out[0], out[1], out[0].T, out[1].T):
        m = m.astype(np.float32)
        hi = m.astype(ml_dtypes.bfloat16)
        lo = (m - hi.astype(np.float32)).astype(ml_dtypes.bfloat16)
        both.append(np.stack([hi, lo]))
    return np.stack(both)


def parity_table(pixels):
    half = pixels // 2
    t = np.zeros((pixels, pixels), np.float32)
    for j in range(half):
        t[2 * j, j] = 1.0
        t[2 * j + 1, half + j] = 1.0
    return t.astype(ml_dtypes.bfloat16)


def split(x):
    hi = x.astype(BF16)
    return hi, (x - hi.astype(F32)).astype(BF16)


def mm(a, b):
    return jnp.dot(a, b, preferred_element_type=F32)


def from_left(table, x):
    hi, lo = split(x)
    return mm(jnp.concatenate([table[0], table[0], table[1]], 1), jnp.concatenate([hi, lo, hi], 0))


def from_right(x, table):
    hi, lo = split(x)
    return mm(jnp.concatenate([hi, lo, hi], 1), jnp.concatenate([table[0], table[0], table[1]], 0))


def step_kernel(pos_ref, count_ref, canvas_ref, probe_ref, amp_ref, tab_ref, par_ref,
                spread_ref, pg_ref, shift_ref, energy_ref,
                win, patch, far, inten, grad, col0, col1):
    n = probe_ref.shape[2]
    h = n // 2
    modes = probe_ref.shape[1]
    slots = amp_ref.shape[0]
    spread_ref[...] = jnp.zeros_like(spread_ref)
    pg_ref[...] = jnp.zeros_like(pg_ref)
    energy_ref[0] = 0.0
    for s in range(slots):
        shift_ref[s, 0] = 0.0
        shift_ref[s, 1] = 0.0

    def visit(s, carry):
        a = pos_ref[s, 0]
        b = pos_ref[s, 1]
        base = pl.multiple_of((b - 1) // 128 * 128, 128)
        turn = (b - 1) % 128
        row = pl.multiple_of((a - 1) // 8 * 8, 8)
        row_turn = (a - 1) % 8
        power = jnp.zeros((1, 1), F32)
        for part in range(2):
            w = canvas_ref[part, pl.ds(row, n + 16), pl.ds(base, 512)]
            w = pltpu.roll(w, 512 - turn, 1)
            w = pltpu.roll(w, n + 16 - row_turn, 0)[:n + 8]
            win[part] = w[:, :384]
            p = pltpu.roll(w, 511, 1)[1:n + 1, :n]
            patch[part] = p
            power += jnp.sum(p * p, keepdims=True)
        energy_ref[0] += power[0, 0] / (n * n)

        inten[...] = jnp.zeros_like(inten)

        def forward(k, c):
            pr, pi = probe_ref[0, k], probe_ref[1, k]
            pr_, pi_ = patch[0], patch[1]
            er = pr * pr_ - pi * pi_
            ei = pr * pi_ + pi * pr_
            up = jnp.concatenate([er[:h] + er[h:], ei[:h] + ei[h:]], 0)
            dn = jnp.concatenate([er[:h] - er[h:], ei[:h] - ei[h:]], 0)
            su = from_left(tab_ref[0], up)
            sd = from_left(tab_ref[1], dn)
            zr = jnp.concatenate([su[:h], sd[:h]], 0)
            zi = jnp.concatenate([su[h:], sd[h:]], 0)
            lf = jnp.concatenate([zr[:, :h] + zr[:, h:], zi[:, :h] + zi[:, h:]], 1)
            rt = jnp.concatenate([zr[:, :h] - zr[:, h:], zi[:, :h] - zi[:, h:]], 1)
            fa = from_right(lf, tab_ref[2])
            fb = from_right(rt, tab_ref[3])
            far[k, 0] = fa
            far[k, 1] = fb
            inten[:, :h] += fa[:, :h] * fa[:, :h] + fa[:, h:] * fa[:, h:]
            inten[:, h:] += fb[:, :h] * fb[:, :h] + fb[:, h:] * fb[:, h:]
            return c

        lax.fori_loop(0, modes, forward, 0)
        hi, lo = split(amp_ref[s])
        am = mm(hi, par_ref[...]) + mm(lo, par_ref[...])
        col0[...] = am[:, :h]
        col1[...] = am[:, h:]
        am = jnp.concatenate([jnp.concatenate([col[pl.ds(p, h, 2), :] for p in range(2)], 0) for col in (col0, col1)], 1)
        inten[...] = am * lax.rsqrt(jnp.maximum(inten[...], INTENSITY_FLOOR)) - 1.0
        grad[...] = jnp.zeros_like(grad)

        def backward(k, c):
            ma, mb = inten[:, :h], inten[:, h:]
            e = from_right(far[k, 0] * jnp.concatenate([ma, ma], 1), tab_ref[0])
            o = from_right(far[k, 1] * jnp.concatenate([mb, mb], 1), tab_ref[1])
            lo = e + o
            hi = e - o
            ev = jnp.concatenate([jnp.concatenate([lo[:h, :h], hi[:h, :h]], 1),
                                  jnp.concatenate([lo[:h, h:], hi[:h, h:]], 1)], 0)
            od = jnp.concatenate([jnp.concatenate([lo[h:, :h], hi[h:, :h]], 1),
                                  jnp.concatenate([lo[h:, h:], hi[h:, h:]], 1)], 0)
            e2 = from_left(tab_ref[2], ev)
            o2 = from_left(tab_ref[3], od)
            for r, half in ((slice(0, h), e2 + o2), (slice(h, n), e2 - o2)):
                cr, ci = half[:h], half[h:]
                pr, pi = probe_ref[0, k, r], probe_ref[1, k, r]
                qr, qi = patch[0, r], patch[1, r]
                grad[0, r] += pr * cr + pi * ci
                grad[1, r] += pr * ci - pi * cr
                pg_ref[0, k, r] += qr * cr + qi * ci
                pg_ref[1, k, r] += qr * ci - qi * cr
            return c

        lax.fori_loop(0, modes, backward, 0)
        along = jnp.zeros((1, 1), F32)
        across = jnp.zeros((1, 1), F32)
        base2 = pl.multiple_of(b // 128 * 128, 128)
        row2 = pl.multiple_of(a // 8 * 8, 8)
        for part in range(2):
            g = grad[part]
            w = win[part]
            mid = pltpu.roll(w, 383, 1)[:, :n]
            along += jnp.sum(g * (mid[2:n + 2] - mid[0:n]), keepdims=True)
            nxt = pltpu.roll(w, 382, 1)[1:n + 1, :n]
            across += jnp.sum(g * (nxt - w[1:n + 1, :n]), keepdims=True)
            g = pltpu.roll(jnp.concatenate([g, jnp.zeros((n, 128), F32)], 1), b % 128, 1)
            g = pltpu.roll(jnp.concatenate([g, jnp.zeros((8, 384), F32)], 0), a % 8, 0)
            spread_ref[part, pl.ds(row2, n + 8), pl.ds(base2, 384)] += g
        shift_ref[s, 0] = along[0, 0] * (0.5 / n)
        shift_ref[s, 1] = across[0, 0] * (0.5 / n)
        return carry

    lax.fori_loop(0, count_ref[0], visit, 0)


def step(pos, count, canvas, probe, amp):
    n = probe.shape[2]
    modes = probe.shape[1]
    slots = amp.shape[0]
    rows = canvas.shape[1] - 8
    vmem = pl.BlockSpec(memory_space=pltpu.VMEM)
    smem = pl.BlockSpec(memory_space=pltpu.SMEM)
    return pl.pallas_call(
        step_kernel,
        out_shape=(
            jax.ShapeDtypeStruct((2, rows, rows), F32),
            jax.ShapeDtypeStruct(probe.shape, F32),
            jax.ShapeDtypeStruct((slots, 2), F32),
            jax.ShapeDtypeStruct((1,), F32),
        ),
        in_specs=[smem, smem, vmem, vmem, vmem, vmem, vmem],
        out_specs=(vmem, vmem, smem, smem),
        scratch_shapes=[
            pltpu.VMEM((2, n + 8, 384), F32),
            pltpu.VMEM((2, n, n), F32),
            pltpu.VMEM((modes, 2, n, n), F32),
            pltpu.VMEM((n, n), F32),
            pltpu.VMEM((2, n, n), F32),
            pltpu.VMEM((n, n // 2), F32),
            pltpu.VMEM((n, n // 2), F32),
        ],
        compiler_params=pltpu.CompilerParams(vmem_limit_bytes=50 * 2**20),
    )(pos, count, canvas, probe, amp, jnp.asarray(dft_tables(n)), jnp.asarray(parity_table(n)))


def body(object_field, probe, amplitudes, positions, counts):
    tile_cells = object_field.shape[1]
    extended = padded(object_field, (("row", 1), ("col", 2)), HALO)
    canvas = jnp.pad(extended, ((0, 0), (0, 8), (0, 128)))
    spread, probe_grad, shift, energy = step(positions[0, 0], counts[0], canvas, probe, amplitudes[0, 0])
    position_grad = shift[None, None]
    summed, total_energy = lax.psum((probe_grad, energy[0]), ("row", "col"))
    probe_new = probe + summed / (total_energy + EPSILON)
    for offset_sign in (1, -1):
        outgoing = spread[:, tile_cells + HALO :, :] if offset_sign == 1 else spread[:, :HALO, :]
        arrived = shifted(outgoing, "row", offset_sign)
        first_row = HALO if offset_sign == 1 else tile_cells
        spread = spread.at[:, first_row : first_row + HALO, :].add(arrived)
    spread = spread[:, HALO : HALO + tile_cells, :]
    for offset_sign in (1, -1):
        outgoing = spread[:, :, tile_cells + HALO :] if offset_sign == 1 else spread[:, :, :HALO]
        arrived = shifted(outgoing, "col", offset_sign)
        first_col = HALO if offset_sign == 1 else tile_cells
        spread = spread.at[:, :, first_col : first_col + HALO].add(arrived)
    folded = spread[:, :, HALO : HALO + tile_cells]
    illumination = jnp.max(jnp.sum(probe * probe, axis=(0, 1)))
    object_new = object_field + folded / illumination
    return (object_new, probe_new, position_grad)


def solution(mesh):
    return jax.shard_map(
        body,
        mesh=mesh,
        in_specs=(
            P(None, "row", "col"),
            P(),
            P("row", "col", None, None, None),
            P("row", "col", None, None),
            P("row", "col"),
        ),
        out_specs=(P(None, "row", "col"), P(), P("row", "col", None, None)),
        check_vma=False,
    )
```

profile of v0, /device:TPU:1, one launch (start us, length us, event | category | flops | bytes accessed | tf_op | source)
XLA Modules:
  0.0 323.1 jit_solution(4627386490412593599)
XLA Ops:
  7.2 0.0 copy-start.3
  7.2 0.0 all-reduce.3.cloned.1.call-start
  7.2 1.4 fusion.5
  8.6 6.0 %collective-permute-start = (f32[2,128,512]{2,1,0:T(8,128)S(1)}, f32[2,128,512]{2,1,0:T(8,128)S(1)}, u32[]{:S(2)}, u32[]{:S(2)}) collective-permute-start(f32[2,128,512]{2,1,0:T(8,128)S(1)} %get-tuple-element.64), channel_id=1, source_target_pairs={{0,8},{8,16},{16,24},{24,32},{32,40},{40,48},{48,56},{56,64},{64,7... | collective-permute-start | bytes 1572872 | tf_op jit(solution)/shard_map/ppermute | solution.py:26
  14.7 1.9 collective-permute-start.1
  16.6 4.2 %collective-permute-done = f32[2,128,512]{2,1,0:T(8,128)S(1)} collective-permute-done((f32[2,128,512]{2,1,0:T(8,128)S(1)}, f32[2,128,512]{2,1,0:T(8,128)S(1)}, u32[]{:S(2)}, u32[]{:S(2)}) %collective-permute-start) | collective-permute-done | bytes 524320 | tf_op jit(solution)/shard_map/ppermute | solution.py:26
  20.8 0.0 copy-done.3
  20.9 0.2 constant_dynamic-update-slice_fusion.1
  21.0 0.0 copy-start.6
  21.0 7.1 %collective-permute-done.1 = f32[2,128,512]{2,1,0:T(8,128)S(1)} collective-permute-done((f32[2,128,512]{2,1,0:T(8,128)S(1)}, f32[2,128,512]{2,1,0:T(8,128)S(1)}, u32[]{:S(2)}, u32[]{:S(2)}) %collective-permute-start.1) | collective-permute-done | bytes 524320 | tf_op jit(solution)/shard_map/ppermute | solution.py:27
  28.1 0.0 copy-start.5
  28.1 1.3 fusion.4
  29.5 3.6 %collective-permute-start.2 = (f32[2,768,128]{2,1,0:T(8,128)}, f32[2,768,128]{2,1,0:T(8,128)S(1)}, u32[]{:S(2)}, u32[]{:S(2)}) collective-permute-start(f32[2,768,128]{2,1,0:T(8,128)} %get-tuple-element.59), channel_id=1, source_target_pairs={{0,1},{1,2},{2,3},{3,4},{4,5},{5,6},{6,7},{8,9},{9,10},{10,11},{11... | collective-permute-start | bytes 2359304 | tf_op jit(solution)/shard_map/ppermute | solution.py:26
  33.1 1.3 collective-permute-start.3
  35.0 0.0 copy-done.5
  35.0 0.0 copy-done.6
  35.0 0.1 copy.12.pos_ref
  35.1 0.0 copy-start
  35.1 0.0 copy-start.1
  35.1 0.0 copy-start.2
  35.1 7.1 %collective-permute-done.2 = f32[2,768,128]{2,1,0:T(8,128)S(1)} collective-permute-done((f32[2,768,128]{2,1,0:T(8,128)}, f32[2,768,128]{2,1,0:T(8,128)S(1)}, u32[]{:S(2)}, u32[]{:S(2)}) %collective-permute-start.2) | collective-permute-done | bytes 786464 | tf_op jit(solution)/shard_map/ppermute | solution.py:26
  42.2 4.0 %collective-permute-done.3 = f32[2,768,128]{2,1,0:T(8,128)} collective-permute-done((f32[2,768,128]{2,1,0:T(8,128)}, f32[2,768,128]{2,1,0:T(8,128)}, u32[]{:S(2)}, u32[]{:S(2)}) %collective-permute-start.3) | collective-permute-done | bytes 786464 | tf_op jit(solution)/shard_map/ppermute | solution.py:27
  46.3 4.2 %select_maximum_fusion.canvas_ref = f32[2,776,896]{2,1,0:T(8,128)} fusion(f32[2,768,128]{2,1,0:T(8,128)} %collective-permute-done.3, f32[2,768,512]{2,1,0:T(8,128)} %copy-done.5, f32[2,768,128]{2,1,0:T(8,128)S(1)} %collective-permute-done.2), kind=kLoop, calls=%fused_computation | loop fusion | flops 15296512 | bytes 10280960 | tf_op jit(solution)/shard_map/concatenate | solution.py:28
  50.4 0.0 copy-done
  50.4 0.0 copy-done.1
  50.4 0.0 copy-done.2
  50.4 52.7 %shard_map.94 = (f32[2,768,768]{2,1,0:T(8,128)}, f32[2,4,256,256]{3,2,1,0:T(8,128)}, f32[6,2]{1,0:T(8,128)S(1)}, f32[1]{0:T(128)}) custom-call(s32[6,2]{1,0:T(8,128)S(1)} %copy.12.pos_ref, s32[1]{0:T(128)} %bitcast.5.count_ref, f32[2,776,896]{2,1,0:T(8,128)} %select_maximum_fusion.canvas_ref, f32[2,4,256,256]{3,2,1,0:T(8,128)} %probe_ref.1, ...), custom_call_target="tpu_custom_call" | custom-call | tf_op jit(solution)/shard_map/pallas_call | solution.py:200
  103.2 1.2 slice.133
  104.4 1.9 collective-permute-start.4
  106.3 8.9 %collective-permute-done.4 = f32[2,128,768]{2,1,0:T(8,128)S(1)} collective-permute-done((f32[2,128,768]{2,1,0:T(8,128)S(1)}, f32[2,128,768]{2,1,0:T(8,128)S(1)}, u32[]{:S(2)}, u32[]{:S(2)}) %collective-permute-start.4) | collective-permute-done | bytes 786464 | tf_op jit(solution)/shard_map/ppermute | solution.py:35
  115.2 2.1 add_dynamic-update-slice_fusion
  117.3 1.2 slice.145
  118.5 1.9 collective-permute-start.5
  120.4 0.0 all-reduce.3.cloned.1.call-update
  120.4 13.7 %collective-permute-done.5 = f32[2,128,768]{2,1,0:T(8,128)} collective-permute-done((f32[2,128,768]{2,1,0:T(8,128)S(1)}, f32[2,128,768]{2,1,0:T(8,128)}, u32[]{:S(2)}, u32[]{:S(2)}) %collective-permute-start.5) | collective-permute-done | bytes 786464 | tf_op jit(solution)/shard_map/ppermute | solution.py:35
  134.2 2.3 fusion.1
  136.5 1.1 slice.148
  137.6 11.0 %collective-permute-start.6 = (f32[2,512,128]{2,1,0:T(8,128)S(1)}, f32[2,512,128]{2,1,0:T(8,128)S(1)}, u32[]{:S(2)}, u32[]{:S(2)}) collective-permute-start(f32[2,512,128]{2,1,0:T(8,128)S(1)} %slice.148), channel_id=1, source_target_pairs={{0,1},{1,2},{2,3},{3,4},{4,5},{5,6},{6,7},{8,9},{9,10},{10,11},{11... | collective-permute-start | bytes 1572872 | tf_op jit(solution)/shard_map/ppermute | solution.py:35
  148.6 2.1 slice.146
  150.7 4.0 %collective-permute-done.6 = f32[2,512,128]{2,1,0:T(8,128)S(1)} collective-permute-done((f32[2,512,128]{2,1,0:T(8,128)S(1)}, f32[2,512,128]{2,1,0:T(8,128)S(1)}, u32[]{:S(2)}, u32[]{:S(2)}) %collective-permute-start.6) | collective-permute-done | bytes 524320 | tf_op jit(solution)/shard_map/ppermute | solution.py:35
  154.7 1.1 fusion.3
  155.8 0.0 copy-start.4
  155.8 1.6 copy-done.4
  157.5 1.3 collective-permute-start.7
  158.8 88.2 %psum.15 = f32[]{:T(128)} all-reduce(f32[]{:T(128)} %bitcast.3), channel_id=1, replica_groups=mesh['row'=16,'col'=8] {'row','col'}, use_global_device_ids=true, to_apply=%region_3.4 | all-reduce | flops 1 | bytes 8 | tf_op jit(solution)/shard_map/psum | solution.py:229
  247.0 0.6 copy.13
  248.3 57.5 %all-reduce.3.cloned.1.call-done = f32[2,4,256,256]{3,2,1,0:T(8,128)} async-done(((f32[2,4,256,256]{3,2,1,0:T(8,128)}), f32[2,4,256,256]{3,2,1,0:T(8,128)}) %all-reduce.3.cloned.1.call-update) | async-done | bytes 2097168 | tf_op jit(solution)/shard_map/psum | solution.py:229
  305.8 3.9 %divide_add_fusion = (f32[2,4,256,256]{3,2,1,0:T(8,128)}, f32[256,256]{1,0:T(8,128)S(1)}) fusion(f32[2,4,256,256]{3,2,1,0:T(8,128)} %probe_ref.1, f32[2,4,256,256]{3,2,1,0:T(8,128)} %all-reduce.3.cloned.1.call-done, f32[]{:T(128)S(6)} %add.48), kind=kLoop, calls=%fused_computation.6 | loop fusion | flops 2031616 | bytes 6553604 | tf_op jit(solution)/shard_map/add | solution.py:230
  309.7 0.7 reduce_max.9
  310.3 0.0 collective-permute-done.7
  310.3 1.9 fusion.2
  312.3 4.0 %fusion = f32[2,512,512]{2,1,0:T(8,128)} fusion(f32[2,512,512]{2,1,0:T(8,128)S(1)} %copy-done.3, f32[2,512,768]{2,1,0:T(8,128)} %fusion.2, f32[]{:T(128)} %reduce_max.9), kind=kLoop, calls=%fused_computation.5 | loop fusion | flops 1048576 | bytes 6291460 | tf_op jit(solution)/shard_map/add | solution.py:244
  (3 shorter events, 0.1 us)
Async XLA Ops:
  7.2 13.7 %copy-start.3 = (f32[2,512,512]{2,1,0:T(8,128)S(1)}, f32[2,512,512]{2,1,0:T(8,128)}, u32[]{:S(2)}) copy-start(f32[2,512,512]{2,1,0:T(8,128)} %param.15) | copy-start | bytes 6291460
  7.2 298.6 %all-reduce.3.cloned.1.call-start = ((), (), s32[]{:S(2)}) async-start(), calls=%async_computation | async-start | bytes 4194304 | tf_op jit(solution)/shard_map/psum | solution.py:229
  8.6 12.2 %collective-permute-start = (f32[2,128,512]{2,1,0:T(8,128)S(1)}, f32[2,128,512]{2,1,0:T(8,128)S(1)}, u32[]{:S(2)}, u32[]{:S(2)}) collective-permute-start(f32[2,128,512]{2,1,0:T(8,128)S(1)} %get-tuple-element.64), channel_id=1, source_target_pairs={{0,8},{8,16},{16,24},{24,32},{32,40},{40,48},{48,56},{56,64},{64,7... | collective-permute-start | bytes 1572872 | tf_op jit(solution)/shard_map/ppermute | solution.py:26
  14.7 13.4 %collective-permute-start.1 = (f32[2,128,512]{2,1,0:T(8,128)S(1)}, f32[2,128,512]{2,1,0:T(8,128)S(1)}, u32[]{:S(2)}, u32[]{:S(2)}) collective-permute-start(f32[2,128,512]{2,1,0:T(8,128)S(1)} %get-tuple-element.63), channel_id=1, source_target_pairs={{8,0},{16,8},{24,16},{32,24},{40,32},{48,40},{56,48},{64,56},{72,6... | collective-permute-start | bytes 1572872 | tf_op jit(solution)/shard_map/ppermute | solution.py:27
  21.0 14.0 %copy-start.6 = (s32[1,1,6,2]{2,3,1,0:T(2,128)S(1)}, s32[1,1,6,2]{2,3,1,0:T(2,128)}, u32[]{:S(2)}) copy-start(s32[1,1,6,2]{2,3,1,0:T(2,128)} %param.18) | copy-start | bytes 148
  28.1 6.9 %copy-start.5 = (f32[2,768,512]{2,1,0:T(8,128)}, f32[2,768,512]{2,1,0:T(8,128)S(1)}, u32[]{:S(2)}) copy-start(f32[2,768,512]{2,1,0:T(8,128)S(1)} %constant_dynamic-update-slice_fusion) | copy-start | bytes 9437188
  29.5 12.8 %collective-permute-start.2 = (f32[2,768,128]{2,1,0:T(8,128)}, f32[2,768,128]{2,1,0:T(8,128)S(1)}, u32[]{:S(2)}, u32[]{:S(2)}) collective-permute-start(f32[2,768,128]{2,1,0:T(8,128)} %get-tuple-element.59), channel_id=1, source_target_pairs={{0,1},{1,2},{2,3},{3,4},{4,5},{5,6},{6,7},{8,9},{9,10},{10,11},{11... | collective-permute-start | bytes 2359304 | tf_op jit(solution)/shard_map/ppermute | solution.py:26
  33.1 13.2 %collective-permute-start.3 = (f32[2,768,128]{2,1,0:T(8,128)}, f32[2,768,128]{2,1,0:T(8,128)}, u32[]{:S(2)}, u32[]{:S(2)}) collective-permute-start(f32[2,768,128]{2,1,0:T(8,128)} %get-tuple-element.60), channel_id=1, source_target_pairs={{1,0},{2,1},{3,2},{4,3},{5,4},{6,5},{7,6},{9,8},{10,9},{11,10},{12... | collective-permute-start | bytes 2359304 | tf_op jit(solution)/shard_map/ppermute | solution.py:27
  35.1 15.3 %copy-start = (f32[1,1,6,256,256]{4,3,2,1,0:T(8,128)S(1)}, f32[1,1,6,256,256]{4,3,2,1,0:T(8,128)}, u32[]{:S(2)}) copy-start(f32[1,1,6,256,256]{4,3,2,1,0:T(8,128)} %param.17) | copy-start | bytes 4718596
  35.1 15.3 %copy-start.1 = (bf16[4,2,256,256]{3,2,1,0:T(8,128)(2,1)S(1)}, bf16[4,2,256,256]{3,2,1,0:T(8,128)(2,1)}, u32[]{:S(2)}) copy-start(bf16[4,2,256,256]{3,2,1,0:T(8,128)(2,1)} %constant.121.clone.tab_ref) | copy-start | bytes 3145732
  35.1 15.3 %copy-start.2 = (bf16[256,256]{1,0:T(8,128)(2,1)S(1)}, bf16[256,256]{1,0:T(8,128)(2,1)}, u32[]{:S(2)}) copy-start(bf16[256,256]{1,0:T(8,128)(2,1)} %constant.122.clone.par_ref) | copy-start | bytes 393220
  104.4 10.8 %collective-permute-start.4 = (f32[2,128,768]{2,1,0:T(8,128)S(1)}, f32[2,128,768]{2,1,0:T(8,128)S(1)}, u32[]{:S(2)}, u32[]{:S(2)}) collective-permute-start(f32[2,128,768]{2,1,0:T(8,128)S(1)} %slice.133), channel_id=1, source_target_pairs={{0,8},{8,16},{16,24},{24,32},{32,40},{40,48},{48,56},{56,64},{64,7... | collective-permute-start | bytes 2359304 | tf_op jit(solution)/shard_map/ppermute | solution.py:35
  118.5 15.7 %collective-permute-start.5 = (f32[2,128,768]{2,1,0:T(8,128)S(1)}, f32[2,128,768]{2,1,0:T(8,128)}, u32[]{:S(2)}, u32[]{:S(2)}) collective-permute-start(f32[2,128,768]{2,1,0:T(8,128)S(1)} %slice.145), channel_id=1, source_target_pairs={{8,0},{16,8},{24,16},{32,24},{40,32},{48,40},{56,48},{64,56},{72,6... | collective-permute-start | bytes 2359304 | tf_op jit(solution)/shard_map/ppermute | solution.py:35
  137.6 17.1 %collective-permute-start.6 = (f32[2,512,128]{2,1,0:T(8,128)S(1)}, f32[2,512,128]{2,1,0:T(8,128)S(1)}, u32[]{:S(2)}, u32[]{:S(2)}) collective-permute-start(f32[2,512,128]{2,1,0:T(8,128)S(1)} %slice.148), channel_id=1, source_target_pairs={{0,1},{1,2},{2,3},{3,4},{4,5},{5,6},{6,7},{8,9},{9,10},{10,11},{11... | collective-permute-start | bytes 1572872 | tf_op jit(solution)/shard_map/ppermute | solution.py:35
  155.8 1.6 copy-start.4
  157.5 152.8 %collective-permute-start.7 = (f32[2,512,128]{2,1,0:T(8,128)S(1)}, f32[2,512,128]{2,1,0:T(8,128)S(1)}, u32[]{:S(2)}, u32[]{:S(2)}) collective-permute-start(f32[2,512,128]{2,1,0:T(8,128)S(1)} %slice.150), channel_id=1, source_target_pairs={{1,0},{2,1},{3,2},{4,3},{5,4},{6,5},{7,6},{9,8},{10,9},{11,10},{12... | collective-permute-start | bytes 1572872 | tf_op jit(solution)/shard_map/ppermute | solution.py:35
Sparse Core Ops, SparseCore 0:
  120.6 185.2 all-reduce.2
where the time goes:
time: 324 us; the launch traced here: 323 us
  waiting for transfers between devices  106 us (33%)
  blocking collectives  88.2 us (27%)
  Pallas kernels  52.7 us (16%)
  starting transfers between devices  29 us (9%)
  other arithmetic  20.2 us (6%)
  between operations  15.5 us (5%)
  local copies, waits for them, and re-layouts  11 us (3%)
    psum x1, blocking collectives, body(): summed, total_energy = lax.psum((probe_grad, energy[0]), ('row', 'col'))  88.2 us
    psum x1, waiting for transfers between devices, body(): summed, total_energy = lax.psum((probe_grad, energy[0]), ('row', 'col'))  57.5 us
    pallas_call x1, Pallas kernels, step(): pl.pallas_call(step_kernel, out_shape=(jax.ShapeDtypeStruct((2, rows, row...  52.7 us
    ppermute x4, waiting for transfers between devices, shifted(): return lax.ppermute(x, axis, pairs)  26.6 us
    ppermute x4, starting transfers between devices, shifted(): return lax.ppermute(x, axis, pairs)  16.1 us
    ppermute x2, waiting for transfers between devices, padded(): before = lax.ppermute(last, axis, up)  11.3 us
    ppermute x2, waiting for transfers between devices, padded(): after = lax.ppermute(first, axis, down)  11.1 us
    ppermute x2, starting transfers between devices, padded(): before = lax.ppermute(last, axis, up)  9.62 us
  transfers between devices with their start and end apart: 9, of which 8 were waited for; matrix products, arithmetic and copies ran while one was open for 4% of the time, Pallas kernels for 0%

commit v1 on v0

--- a/solution.py
+++ b/solution.py
@@ -1,3 +1,4 @@
+import functools
 import math
 
 import ml_dtypes
@@ -14,25 +15,6 @@
 EPSILON = 1e-06
 F32 = jnp.float32
 BF16 = jnp.bfloat16
-
-
-def padded(x, sides, width):
-    for axis, dim in sides:
-        peers, length = (lax.axis_size(axis), x.shape[dim])
-        up = [(i, (i + 1) % peers) for i in range(peers - 1)]
-        down = [(j, i) for i, j in up]
-        last = lax.slice_in_dim(x, length - width, length, axis=dim)
-        first = lax.slice_in_dim(x, 0, width, axis=dim)
-        before = lax.ppermute(last, axis, up)
-        after = lax.ppermute(first, axis, down)
-        x = jnp.concatenate([before, x, after], axis=dim)
-    return x
-
-
-def shifted(x, axis, by):
-    peers = lax.axis_size(axis)
-    pairs = [(i, i + by) for i in range(peers) if 0 <= i + by < peers]
-    return lax.ppermute(x, axis, pairs)
 
 
 def dft_tables(pixels):
@@ -83,7 +65,7 @@
 
 
 def step_kernel(pos_ref, count_ref, canvas_ref, probe_ref, amp_ref, tab_ref, par_ref,
-                spread_ref, pg_ref, shift_ref, energy_ref,
+                spread_ref, pg_ref, shift_ref, energy_ref, illum_ref,
                 win, patch, far, inten, grad, col0, col1):
     n = probe_ref.shape[2]
     h = n // 2
@@ -91,7 +73,12 @@
     slots = amp_ref.shape[0]
     spread_ref[...] = jnp.zeros_like(spread_ref)
     pg_ref[...] = jnp.zeros_like(pg_ref)
-    energy_ref[0] = 0.0
+    energy_ref[...] = jnp.zeros_like(energy_ref)
+    light = jnp.zeros((n, n), F32)
+    for k in range(modes):
+        for part in range(2):
+            light += probe_ref[part, k] * probe_ref[part, k]
+    illum_ref[0] = jnp.max(light)
     for s in range(slots):
         shift_ref[s, 0] = 0.0
         shift_ref[s, 1] = 0.0
@@ -112,7 +99,7 @@
             p = pltpu.roll(w, 511, 1)[1:n + 1, :n]
             patch[part] = p
             power += jnp.sum(p * p, keepdims=True)
-        energy_ref[0] += power[0, 0] / (n * n)
+        energy_ref[...] += power / (n * n)
 
         inten[...] = jnp.zeros_like(inten)
 
@@ -203,10 +190,11 @@
             jax.ShapeDtypeStruct((2, rows, rows), F32),
             jax.ShapeDtypeStruct(probe.shape, F32),
             jax.ShapeDtypeStruct((slots, 2), F32),
+            jax.ShapeDtypeStruct((8, n), F32),
             jax.ShapeDtypeStruct((1,), F32),
         ),
         in_specs=[smem, smem, vmem, vmem, vmem, vmem, vmem],
-        out_specs=(vmem, vmem, smem, smem),
+        out_specs=(vmem, vmem, smem, vmem, smem),
         scratch_shapes=[
             pltpu.VMEM((2, n + 8, 384), F32),
             pltpu.VMEM((2, n, n), F32),
@@ -220,34 +208,274 @@
     )(pos, count, canvas, probe, amp, jnp.asarray(dft_tables(n)), jnp.asarray(parity_table(n)))
 
 
-def body(object_field, probe, amplitudes, positions, counts):
-    tile_cells = object_field.shape[1]
-    extended = padded(object_field, (("row", 1), ("col", 2)), HALO)
-    canvas = jnp.pad(extended, ((0, 0), (0, 8), (0, 128)))
-    spread, probe_grad, shift, energy = step(positions[0, 0], counts[0], canvas, probe, amplitudes[0, 0])
-    position_grad = shift[None, None]
-    summed, total_energy = lax.psum((probe_grad, energy[0]), ("row", "col"))
-    probe_new = probe + summed / (total_energy + EPSILON)
-    for offset_sign in (1, -1):
-        outgoing = spread[:, tile_cells + HALO :, :] if offset_sign == 1 else spread[:, :HALO, :]
-        arrived = shifted(outgoing, "row", offset_sign)
-        first_row = HALO if offset_sign == 1 else tile_cells
-        spread = spread.at[:, first_row : first_row + HALO, :].add(arrived)
-    spread = spread[:, HALO : HALO + tile_cells, :]
-    for offset_sign in (1, -1):
-        outgoing = spread[:, :, tile_cells + HALO :] if offset_sign == 1 else spread[:, :, :HALO]
-        arrived = shifted(outgoing, "col", offset_sign)
-        first_col = HALO if offset_sign == 1 else tile_cells
-        spread = spread.at[:, :, first_col : first_col + HALO].add(arrived)
-    folded = spread[:, :, HALO : HALO + tile_cells]
-    illumination = jnp.max(jnp.sum(probe * probe, axis=(0, 1)))
-    object_new = object_field + folded / illumination
-    return (object_new, probe_new, position_grad)
+MESH = pl.DeviceIdType.MESH
+SIDES = [(-1, 0), (1, 0), (0, -1), (0, 1), (-1, -1), (-1, 1), (1, -1), (1, 1)]
+
+
+def place():
+    return lax.axis_index("row"), lax.axis_index("col")
+
+
+def present(side, limits):
+    row, col = place()
+    fits = None
+    for at, by, limit in ((row, side[0], limits[0]), (col, side[1], limits[1])):
+        if by:
+            ok = at > 0 if by < 0 else at < limit - 1
+            fits = ok if fits is None else jnp.logical_and(fits, ok)
+    return fits
+
+
+def neighbour(side):
+    row, col = place()
+    return (row + side[0], col + side[1])
+
+
+def edge(by, cells):
+    return pl.ds(0, cells) if by == 0 else (pl.ds(0, HALO) if by < 0 else pl.ds(cells - HALO, HALO))
+
+
+def rim(by, cells):
+    return pl.ds(HALO, cells) if by == 0 else (pl.ds(0, HALO) if by < 0 else pl.ds(cells + HALO, HALO))
+
+
+def greet_sides(limits):
+    barrier = pltpu.get_barrier_semaphore()
+    total = jnp.int32(0)
+    for side in SIDES:
+        here = present(side, limits)
+        total += here.astype(jnp.int32)
+
+        @pl.when(here)
+        def _():
+            pl.semaphore_signal(barrier, inc=1, device_id=neighbour(side), device_id_type=MESH)
+
+    return barrier, total
+
+
+def halo_kernel(limits, obj_ref, canvas_ref, zeros, own_sem, zero_sems, send_sems, recv_sems):
+    cells = obj_ref.shape[1]
+    barrier, total = greet_sides(limits)
+    own = pltpu.make_async_copy(obj_ref, canvas_ref.at[:, pl.ds(HALO, cells), pl.ds(HALO, cells)], own_sem)
+    own.start()
+    zeros[...] = jnp.zeros_like(zeros)
+    pl.semaphore_wait(barrier, total)
+    steps = []
+    for i, side in enumerate(SIDES):
+        here = present(side, limits)
+        back = SIDES.index((-side[0], -side[1]))
+        send = pltpu.make_async_remote_copy(
+            src_ref=obj_ref.at[:, edge(side[0], cells), edge(side[1], cells)],
+            dst_ref=canvas_ref.at[:, rim(-side[0], cells), rim(-side[1], cells)],
+            send_sem=send_sems.at[i],
+            recv_sem=recv_sems.at[back],
+            device_id=neighbour(side),
+            device_id_type=MESH,
+        )
+        landed = canvas_ref.at[:, rim(side[0], cells), rim(side[1], cells)]
+        tall, wide = (cells if side[0] == 0 else HALO), (cells if side[1] == 0 else HALO)
+        blank = pltpu.make_async_copy(zeros.at[:, pl.ds(0, tall), pl.ds(0, wide)], landed, zero_sems.at[i])
+        arrive = pltpu.make_async_copy(landed, landed, recv_sems.at[i])
+        steps.append((here, send, blank, arrive))
+
+        @pl.when(here)
+        def _(send=send):
+            send.start()
+
+        @pl.when(jnp.logical_not(here))
+        def _(blank=blank):
+            blank.start()
+
+    for here, send, blank, arrive in steps:
+        @pl.when(here)
+        def _(send=send, arrive=arrive):
+            send.wait_send()
+            arrive.wait()
+
+        @pl.when(jnp.logical_not(here))
+        def _(blank=blank):
+            blank.wait()
+
+    own.wait()
+
+
+def exchange_halo(obj, limits):
+    cells = obj.shape[1]
+    return pl.pallas_call(
+        functools.partial(halo_kernel, limits),
+        out_shape=jax.ShapeDtypeStruct((2, cells + 2 * HALO + 8, cells + 3 * HALO), F32),
+        in_specs=[pl.BlockSpec(memory_space=pl.ANY)],
+        out_specs=pl.BlockSpec(memory_space=pl.ANY),
+        scratch_shapes=[
+            pltpu.VMEM((2, cells, cells), F32),
+            pltpu.SemaphoreType.DMA,
+            pltpu.SemaphoreType.DMA((8,)),
+            pltpu.SemaphoreType.DMA((8,)),
+            pltpu.SemaphoreType.DMA((8,)),
+        ],
+        compiler_params=pltpu.CompilerParams(collective_id=0, has_side_effects=True, vmem_limit_bytes=16 * 2**20),
+    )(obj)
+
+
+def finish_kernel(limits, spread_ref, pg_ref, energy_ref, obj_ref, probe_ref, illum_ref,
+                  onew_ref, pnew_ref, land_rows, land_cols, land_corners, mate_half, mate_energy, outbox, inbox,
+                  fold_send, fold_recv, mate_send, mate_recv, bulk):
+    cells = obj_ref.shape[1]
+    row, col = place()
+    core = row % 2
+    mate = (row + 1 - 2 * core, col)
+    pairs, cols = limits[0] // 2, limits[1]
+    chips = pairs * cols
+    me = row // 2 * cols + col
+    chunk = pg_ref.shape[1] // chips
+
+    def peer(d):
+        pair = (row // 2 + d // cols) % pairs
+        at = (col + d % cols) % cols
+        return pair * cols + at, (2 * pair + core, at)
+
+    barrier, total = greet_sides(limits)
+
+    def greet(d, c):
+        pl.semaphore_signal(barrier, inc=1, device_id=peer(d)[1], device_id_type=MESH)
+        return c
+
+    pl.semaphore_signal(barrier, inc=1, device_id=mate, device_id_type=MESH)
+    lax.fori_loop(1, chips, greet, 0)
+    pl.semaphore_wait(barrier, total + chips)
+
+    def to_mate(src, dst, i):
+        return pltpu.make_async_remote_copy(src_ref=src, dst_ref=dst, send_sem=mate_send.at[i], recv_sem=mate_recv.at[i],
+                                            device_id=mate, device_id_type=MESH)
+
+    first = to_mate(pg_ref.at[1 - core], mate_half, 0)
+    second = to_mate(energy_ref, mate_energy, 1)
+    first.start()
+    second.start()
+    first.wait()
+    second.wait()
+    warm = energy_ref[...] + mate_energy[...]
+
+    def pack(q, c):
+        rows = pl.ds(pl.multiple_of(q * chunk, chunk), chunk)
+        outbox[q, pl.ds(0, chunk), :] = pg_ref[core, rows, :] + mate_half[rows, :]
+        outbox[q, pl.ds(chunk, 8), :] = warm
+        return c
+
+    lax.fori_loop(0, chips, pack, 0)
+
+    def scatter(d, c):
+        q, device = peer(d)
+        pltpu.make_async_remote_copy(src_ref=outbox.at[q], dst_ref=inbox.at[d - 1], send_sem=bulk.at[0], recv_sem=bulk.at[1],
+                                     device_id=device, device_id_type=MESH).start()
+        return c
+
+    lax.fori_loop(1, chips, scatter, 0)
+
+    folds = []
+    for i, side in enumerate(SIDES):
+        here = present(side, limits)
+        back = SIDES.index((-side[0], -side[1]))
+        land = land_rows.at[back] if i < 2 else land_cols.at[back - 2] if i < 4 else land_corners.at[back - 4]
+        send = pltpu.make_async_remote_copy(
+            src_ref=spread_ref.at[:, rim(side[0], cells), rim(side[1], cells)],
+            dst_ref=land,
+            send_sem=fold_send.at[i],
+            recv_sem=fold_recv.at[back],
+            device_id=neighbour(side),
+            device_id_type=MESH,
+        )
+        mine = land_rows.at[i] if i < 2 else land_cols.at[i - 2] if i < 4 else land_corners.at[i - 4]
+        arrive = pltpu.make_async_copy(mine, mine, fold_recv.at[i])
+        folds.append((here, send, arrive, side, mine))
+
+        @pl.when(here)
+        def _(send=send):
+            send.start()
+
+    lower = inbox.at[pl.ds(0, chips - 1)]
+    pltpu.make_async_copy(lower, lower, bulk.at[0]).wait()
+    pltpu.make_async_copy(lower, lower, bulk.at[1]).wait()
+    summed = lax.fori_loop(0, chips - 1, lambda d, c: c + inbox[d], outbox[me])
+    here_rows = pl.ds(pl.multiple_of(me * chunk, chunk), chunk)
+    pnew_ref[core, here_rows, :] = probe_ref[core, here_rows, :] + summed[:chunk] / (summed[chunk:chunk + 1] + EPSILON)
+    out = pnew_ref.at[core, here_rows]
+
+    def gather(d, c):
+        pltpu.make_async_remote_copy(src_ref=out, dst_ref=out, send_sem=bulk.at[2], recv_sem=bulk.at[3],
+                                     device_id=peer(d)[1], device_id_type=MESH).start()
+        return c
+
+    lax.fori_loop(1, chips, gather, 0)
+
+    share = 1.0 / illum_ref[0]
+    step_rows = 64
+
+    def base(j, c):
+        r = pl.ds(pl.multiple_of(j * step_rows, step_rows), step_rows)
+        rr = pl.ds(pl.multiple_of(j * step_rows + HALO, step_rows), step_rows)
+        for part in range(2):
+            onew_ref[part, r, :] = obj_ref[part, r, :] + spread_ref[part, rr, HALO:HALO + cells] * share
+        return c
+
+    lax.fori_loop(0, cells // step_rows, base, 0)
+    for here, send, arrive, side, mine in folds:
+        @pl.when(here)
+        def _(send=send, arrive=arrive, side=side, mine=mine):
+            send.wait_send()
+            arrive.wait()
+            for part in range(2):
+                onew_ref[part, edge(side[0], cells), edge(side[1], cells)] += mine[part] * share
+
+    rest = pnew_ref.at[core, pl.ds(0, (chips - 1) * chunk)]
+    pltpu.make_async_copy(rest, rest, bulk.at[2]).wait()
+    pltpu.make_async_copy(rest, rest, bulk.at[3]).wait()
+    last = to_mate(pnew_ref.at[core], pnew_ref.at[core], 2)
+    last.start()
+    last.wait()
+
+
+def finish(spread, pg, energy, obj, probe, illum, limits):
+    cells = obj.shape[1]
+    rows, lanes = probe.shape[1], probe.shape[2]
+    chips = limits[0] * limits[1] // 2
+    chunk = rows // chips
+    vmem = pl.BlockSpec(memory_space=pltpu.VMEM)
+    return pl.pallas_call(
+        functools.partial(finish_kernel, limits),
+        out_shape=(jax.ShapeDtypeStruct(obj.shape, F32), jax.ShapeDtypeStruct(probe.shape, F32)),
+        in_specs=[vmem, vmem, vmem, vmem, vmem, pl.BlockSpec(memory_space=pltpu.SMEM)],
+        out_specs=(vmem, vmem),
+        scratch_shapes=[
+            pltpu.VMEM((2, 2, HALO, cells), F32),
+            pltpu.VMEM((2, 2, cells, HALO), F32),
+            pltpu.VMEM((4, 2, HALO, HALO), F32),
+            pltpu.VMEM((rows, lanes), F32),
+            pltpu.VMEM((8, lanes), F32),
+            pltpu.VMEM((chips, chunk + 8, lanes), F32),
+            pltpu.VMEM((chips, chunk + 8, lanes), F32),
+            pltpu.SemaphoreType.DMA((8,)),
+            pltpu.SemaphoreType.DMA((8,)),
+            pltpu.SemaphoreType.DMA((3,)),
+            pltpu.SemaphoreType.DMA((3,)),
+            pltpu.SemaphoreType.DMA((4,)),
+        ],
+        compiler_params=pltpu.CompilerParams(collective_id=1, has_side_effects=True, vmem_limit_bytes=40 * 2**20),
+    )(spread, pg, energy, obj, probe, illum)
+
+
+def body(limits, object_field, probe, amplitudes, positions, counts):
+    canvas = exchange_halo(object_field, limits)
+    spread, probe_grad, shift, energy, illum = step(positions[0, 0], counts[0], canvas, probe, amplitudes[0, 0])
+    n = probe.shape[2]
+    flat = (2, probe.shape[1] * n, n)
+    object_new, probe_new = finish(spread, probe_grad.reshape(flat), energy, object_field, probe.reshape(flat), illum, limits)
+    return (object_new, probe_new.reshape(probe.shape), shift[None, None])
 
 
 def solution(mesh):
     return jax.shard_map(
-        body,
+        functools.partial(body, (mesh.shape["row"], mesh.shape["col"])),
         mesh=mesh,
         in_specs=(
             P(None, "row", "col"),

time: 324 us -> 203 us (0.63)
  Pallas kernels: 52.7 us -> 188 us
  waiting for transfers between devices: 106 us -> 0 us
  blocking collectives: 88.2 us -> 0 us
  starting transfers between devices: 29 us -> 0 us
  other arithmetic: 20.2 us -> 0 us
  between operations: 15.5 us -> 1.36 us
    pallas_call x0 -> x2, Pallas kernels: none -> 144 us  [the longest x1 122 us: finish(): pl.pallas_call(functools.partial(finish_kernel, limits), out_shape=(jax.S...]
    psum x1 -> x0, blocking collectives: 88.2 us -> none  [body(): summed, total_energy = lax.psum((probe_grad, energy[0]), ('row', 'col'))]
    psum x1 -> x0, waiting for transfers between devices: 57.5 us -> none  [body(): summed, total_energy = lax.psum((probe_grad, energy[0]), ('row', 'col'))]
    ppermute x8 -> x0, waiting for transfers between devices: 49 us -> none  [the longest x4 26.6 us: shifted(): return lax.ppermute(x, axis, pairs)]
    ppermute x8 -> x0, starting transfers between devices: 29 us -> none  [the longest x4 16.1 us: shifted(): return lax.ppermute(x, axis, pairs)]
    unnamed x16 -> x20, local copies, waits for them, and re-layouts: 1.86 us -> 11.3 us
    pallas_call x1, Pallas kernels: 52.7 us -> 43.8 us  [step(): pl.pallas_call(step_kernel, out_shape=(jax.ShapeDtypeStruct((2, rows, row...]
    slice x7 -> x0, local copies, waits for them, and re-layouts: 8.35 us -> none  [the longest x1 2.1 us: body(): spread = spread[:, HALO:HALO + tile_cells, :]]
  transfers between devices with their start and end apart: 9 -> 0, of which waited for: 8 -> 0; matrix products, arithmetic and copies ran while one was open for 4% -> 0% of each run, Pallas kernels for 0% -> 0%
where the time goes in v1:
time: 203 us; the launch traced here: 202 us
  Pallas kernels  188 us (93%)
  local copies, waits for them, and re-layouts  12.7 us (6%)
    pallas_call x1, Pallas kernels, finish(): pl.pallas_call(functools.partial(finish_kernel, limits), out_shape=(jax.S...  122 us
    pallas_call x1, Pallas kernels, step(): pl.pallas_call(step_kernel, out_shape=(jax.ShapeDtypeStruct((2, rows, row...  43.8 us
    pallas_call x1, Pallas kernels, exchange_halo(): pl.pallas_call(functools.partial(halo_kernel, limits), out_shape=jax.Shap...  22.6 us
    unnamed x20, local copies, waits for them, and re-layouts  11.3 us

profile of v1, /device:TPU:1, one launch (start us, length us, event | category | flops | bytes accessed | tf_op | source)
XLA Modules:
  0.0 202.1 jit_solution(13394529280955038741)
XLA Ops:
  1.3 0.8 copy.10.pos_ref
  2.0 0.0 copy-start.1
  2.0 1.6 copy-done.1
  3.6 0.0 copy-start.6
  3.6 0.0 copy-start.7
  3.6 0.0 copy-start.8
  3.6 22.6 %shard_map.94.canvas_ref = f32[2,776,896]{2,1,0:T(8,128)S(1)} custom-call(f32[2,512,512]{2,1,0:T(8,128)S(1)} %copy-done.1), custom_call_target="tpu_custom_call" | custom-call | tf_op jit(solution)/shard_map/pallas_call | solution.py:304
  26.3 0.0 copy-start
  26.3 2.4 %copy-done = f32[2,776,896]{2,1,0:T(8,128)} copy-done((f32[2,776,896]{2,1,0:T(8,128)}, f32[2,776,896]{2,1,0:T(8,128)S(1)}, u32[]{:S(2)}) %copy-start) | copy-done | bytes 5562392
  28.7 0.0 copy-done.6
  28.7 0.0 copy-done.7
  28.7 0.0 copy-done.8
  28.7 0.0 copy-start.2
  28.7 0.0 copy-start.3
  28.7 43.8 %shard_map.95 = (f32[2,768,768]{2,1,0:T(8,128)}, f32[2,4,256,256]{3,2,1,0:T(8,128)}, f32[6,2]{1,0:T(8,128)S(1)}, f32[8,256]{1,0:T(8,128)S(1)}, f32[1]{0:T(128)}) custom-call(s32[6,2]{1,0:T(8,128)S(1)} %copy.10.pos_ref, s32[1]{0:T(128)} %bitcast.7.count_ref, f32[2,776,896]{2,1,0:T(8,128)} %copy-done, f32[2,4,256,256]{3,2,1,0:T(8,128)} %probe_ref.1, ...), custom_call_target="tpu_custom_call" | custom-call | tf_op jit(solution)/shard_map/pallas_call | solution.py:187
  72.5 0.0 copy-done.2
  72.5 0.0 copy-done.3
  72.5 0.0 copy-start.4
  72.5 1.6 copy-done.4
  74.1 121.6 %shard_map.96 = (f32[2,512,512]{2,1,0:T(8,128)S(1)}, f32[2,1024,256]{2,1,0:T(8,128)S(1)}) custom-call(f32[2,768,768]{2,1,0:T(8,128)} %get-tuple-element.10.spread_ref, f32[2,1024,256]{2,1,0:T(8,128)S(1)} %bitcast.9, f32[8,256]{1,0:T(8,128)S(1)} %get-tuple-element.12.energy_ref, f32[2,512,512]{2,1,0:T(8,128)S(1)} %copy-done.2, f32[2,1024,256]{2,1,0:T(8,128)S(1)} %bitcast.8, ...), custom_call_target="tpu_custom_call" | custom-call | tf_op jit(solution)/shard_map/pallas_call | solution.py:444
  195.8 0.0 copy-start.5
  195.8 1.3 copy-done.5
  197.1 0.6 copy.11
  197.7 3.1 %copy.15 = f32[2,512,512]{2,1,0:T(8,128)} copy(f32[2,512,512]{2,1,0:T(8,128)} %copy-done.5) | data formatting | bytes 4194304
  200.8 1.3 copy.16
Async XLA Ops:
  2.0 1.6 copy-start.1
  3.6 25.0 %copy-start.6 = (f32[1,1,6,256,256]{4,3,2,1,0:T(8,128)S(1)}, f32[1,1,6,256,256]{4,3,2,1,0:T(8,128)}, u32[]{:S(2)}) copy-start(f32[1,1,6,256,256]{4,3,2,1,0:T(8,128)} %param.9) | copy-start | bytes 4718596
  3.6 25.0 %copy-start.7 = (bf16[4,2,256,256]{3,2,1,0:T(8,128)(2,1)S(1)}, bf16[4,2,256,256]{3,2,1,0:T(8,128)(2,1)}, u32[]{:S(2)}) copy-start(bf16[4,2,256,256]{3,2,1,0:T(8,128)(2,1)} %constant.4.clone.tab_ref) | copy-start | bytes 3145732
  3.6 25.0 %copy-start.8 = (bf16[256,256]{1,0:T(8,128)(2,1)S(1)}, bf16[256,256]{1,0:T(8,128)(2,1)}, u32[]{:S(2)}) copy-start(bf16[256,256]{1,0:T(8,128)(2,1)} %constant.5.clone.par_ref) | copy-start | bytes 393220
  26.3 2.4 %copy-start = (f32[2,776,896]{2,1,0:T(8,128)}, f32[2,776,896]{2,1,0:T(8,128)S(1)}, u32[]{:S(2)}) copy-start(f32[2,776,896]{2,1,0:T(8,128)S(1)} %shard_map.94.canvas_ref) | copy-start | bytes 16687108
  28.7 43.8 %copy-start.2 = (f32[2,512,512]{2,1,0:T(8,128)S(1)}, f32[2,512,512]{2,1,0:T(8,128)}, u32[]{:S(2)}) copy-start(f32[2,512,512]{2,1,0:T(8,128)} %obj_ref.3) | copy-start | bytes 6291460
  28.7 43.8 %copy-start.3 = (f32[2,4,256,256]{3,2,1,0:T(8,128)S(1)}, f32[2,4,256,256]{3,2,1,0:T(8,128)}, u32[]{:S(2)}) copy-start(f32[2,4,256,256]{3,2,1,0:T(8,128)} %probe_ref.1) | copy-start | bytes 6291460
  72.5 1.6 copy-start.4
  195.8 1.3 copy-start.5

commit v2 on v1

--- a/solution.py
+++ b/solution.py
@@ -15,6 +15,7 @@
 EPSILON = 1e-06
 F32 = jnp.float32
 BF16 = jnp.bfloat16
+UNROLL = 4
 
 
 def dft_tables(pixels):
@@ -64,42 +65,95 @@
     return mm(jnp.concatenate([hi, lo, hi], 1), jnp.concatenate([table[0], table[0], table[1]], 0))
 
 
+def lane_of():
+    return lax.broadcasted_iota(jnp.int32, (1, 8, 128), 2)
+
+
+def row_of():
+    return lax.broadcasted_iota(jnp.int32, (1, 8, 128), 1)
+
+
+def cut(canvas_ref, patch, a, b):
+    n = patch.shape[1]
+    groups = n // 8
+    t, u = b % 128, a % 8
+    row = pl.multiple_of(a - u, 8)
+    lane, sub = lane_of(), row_of()
+    power = jnp.zeros((8, 128), F32)
+    for part in range(2):
+        blocks = []
+        for j in range(n // 128 + 1):
+            v = canvas_ref[part, pl.ds(row, n + 8), pl.ds(pl.multiple_of(b - t + j * 128, 128), 128)]
+            v = pltpu.roll(v.reshape(groups + 1, 8, 128), (8 - u) % 8, 1)
+            v = jnp.where(sub < 8 - u, v[:groups], v[1:])
+            blocks.append(pltpu.roll(v, (128 - t) % 128, 2))
+        for j in range(n // 128):
+            p = jnp.where(lane < 128 - t, blocks[j], blocks[j + 1])
+            power += jnp.sum(p * p, axis=0)
+            patch[part, :, j * 128:(j + 1) * 128] = p.reshape(n, 128)
+    return power
+
+
+def lay(canvas_ref, spread_ref, grad, a, b):
+    n = grad.shape[1]
+    groups = n // 8
+    count = n // 128
+    t, u = b % 128, a % 8
+    row = pl.multiple_of(a - u, 8)
+    before = pl.multiple_of(jnp.maximum(a - u - 8, 0), 8)
+    lane, sub = lane_of(), row_of()
+    down = jnp.zeros((8, 128), F32)
+    across = jnp.zeros((8, 128), F32)
+    none = jnp.zeros((1, 8, 128), F32)
+    for part in range(2):
+        turned = [pltpu.roll(grad[part, :, j * 128:(j + 1) * 128].reshape(groups, 8, 128), t, 2) for j in range(count)]
+        strips = []
+        for j in range(-1, count + 1):
+            at = pl.multiple_of(jnp.maximum(b - t + j * 128, 0), 128)
+            strips.append(canvas_ref[part, pl.ds(row, n + 8), pl.ds(at, 128)].reshape(groups + 1, 8, 128))
+        for j in range(count + 1):
+            left = turned[j - 1] if j else 0.0
+            g = jnp.where(lane < t, left, turned[j] if j < count else 0.0)
+            g = pltpu.roll(g, u, 1)
+            g = jnp.where(sub < u, jnp.concatenate([none, g], 0), jnp.concatenate([g, none], 0))
+            at = pl.ds(pl.multiple_of(b - t + j * 128, 128), 128)
+            spread_ref[part, pl.ds(row, n + 8), at] += g.reshape(n + 8, 128)
+            v = strips[j + 1]
+            first = canvas_ref[part, pl.ds(before, 8), at].reshape(1, 8, 128)
+            nxt = pltpu.roll(v, 7, 1)
+            prv = pltpu.roll(jnp.concatenate([first, v], 0), 1, 1)
+            nxt = jnp.where(sub < 7, nxt, jnp.concatenate([nxt[1:], none], 0))
+            prv = jnp.where(sub < 1, prv[:-1], prv[1:])
+            down += jnp.sum(g * (nxt - prv), axis=0)
+            nxt = pltpu.roll(v, 127, 2)
+            prv = pltpu.roll(v, 1, 2)
+            if j < count:
+                nxt = jnp.where(lane < 127, nxt, pltpu.roll(strips[j + 2], 127, 2))
+            prv = jnp.where(lane < 1, pltpu.roll(strips[j], 1, 2), prv)
+            across += jnp.sum(g * (nxt - prv), axis=0)
+    return down, across
+
+
 def step_kernel(pos_ref, count_ref, canvas_ref, probe_ref, amp_ref, tab_ref, par_ref,
                 spread_ref, pg_ref, shift_ref, energy_ref, illum_ref,
-                win, patch, far, inten, grad, col0, col1):
+                patch, far, inten, grad, col0, col1, sums):
     n = probe_ref.shape[2]
     h = n // 2
     modes = probe_ref.shape[1]
     slots = amp_ref.shape[0]
     spread_ref[...] = jnp.zeros_like(spread_ref)
     pg_ref[...] = jnp.zeros_like(pg_ref)
-    energy_ref[...] = jnp.zeros_like(energy_ref)
+    sums[...] = jnp.zeros_like(sums)
     light = jnp.zeros((n, n), F32)
     for k in range(modes):
         for part in range(2):
             light += probe_ref[part, k] * probe_ref[part, k]
     illum_ref[0] = jnp.max(light)
-    for s in range(slots):
-        shift_ref[s, 0] = 0.0
-        shift_ref[s, 1] = 0.0
 
     def visit(s, carry):
         a = pos_ref[s, 0]
         b = pos_ref[s, 1]
-        base = pl.multiple_of((b - 1) // 128 * 128, 128)
-        turn = (b - 1) % 128
-        row = pl.multiple_of((a - 1) // 8 * 8, 8)
-        row_turn = (a - 1) % 8
-        power = jnp.zeros((1, 1), F32)
-        for part in range(2):
-            w = canvas_ref[part, pl.ds(row, n + 16), pl.ds(base, 512)]
-            w = pltpu.roll(w, 512 - turn, 1)
-            w = pltpu.roll(w, n + 16 - row_turn, 0)[:n + 8]
-            win[part] = w[:, :384]
-            p = pltpu.roll(w, 511, 1)[1:n + 1, :n]
-            patch[part] = p
-            power += jnp.sum(p * p, keepdims=True)
-        energy_ref[...] += power / (n * n)
+        sums[s, 2] = cut(canvas_ref, patch, a, b)
 
         inten[...] = jnp.zeros_like(inten)
 
@@ -124,7 +178,7 @@
             inten[:, h:] += fb[:, :h] * fb[:, :h] + fb[:, h:] * fb[:, h:]
             return c
 
-        lax.fori_loop(0, modes, forward, 0)
+        lax.fori_loop(0, modes, forward, 0, unroll=UNROLL)
         hi, lo = split(amp_ref[s])
         am = mm(hi, par_ref[...]) + mm(lo, par_ref[...])
         col0[...] = am[:, :h]
@@ -155,33 +209,26 @@
                 pg_ref[1, k, r] += qr * ci - qi * cr
             return c
 
-        lax.fori_loop(0, modes, backward, 0)
-        along = jnp.zeros((1, 1), F32)
-        across = jnp.zeros((1, 1), F32)
-        base2 = pl.multiple_of(b // 128 * 128, 128)
-        row2 = pl.multiple_of(a // 8 * 8, 8)
-        for part in range(2):
-            g = grad[part]
-            w = win[part]
-            mid = pltpu.roll(w, 383, 1)[:, :n]
-            along += jnp.sum(g * (mid[2:n + 2] - mid[0:n]), keepdims=True)
-            nxt = pltpu.roll(w, 382, 1)[1:n + 1, :n]
-            across += jnp.sum(g * (nxt - w[1:n + 1, :n]), keepdims=True)
-            g = pltpu.roll(jnp.concatenate([g, jnp.zeros((n, 128), F32)], 1), b % 128, 1)
-            g = pltpu.roll(jnp.concatenate([g, jnp.zeros((8, 384), F32)], 0), a % 8, 0)
-            spread_ref[part, pl.ds(row2, n + 8), pl.ds(base2, 384)] += g
-        shift_ref[s, 0] = along[0, 0] * (0.5 / n)
-        shift_ref[s, 1] = across[0, 0] * (0.5 / n)
+        lax.fori_loop(0, modes, backward, 0, unroll=UNROLL)
+        down, across = lay(canvas_ref, spread_ref, grad, a, b)
+        sums[s, 0] = down
+        sums[s, 1] = across
         return carry
 
     lax.fori_loop(0, count_ref[0], visit, 0)
+    energy = jnp.zeros((8, 128), F32)
+    for s in range(slots):
+        energy += sums[s, 2]
+        for kind in range(2):
+            shift_ref[s, kind] = jnp.sum(sums[s, kind]) * (0.5 / n)
+    energy_ref[...] = jnp.broadcast_to(jnp.sum(energy, keepdims=True) / (n * n), energy.shape)
 
 
 def step(pos, count, canvas, probe, amp):
     n = probe.shape[2]
     modes = probe.shape[1]
     slots = amp.shape[0]
-    rows = canvas.shape[1] - 8
+    rows = canvas.shape[1]
     vmem = pl.BlockSpec(memory_space=pltpu.VMEM)
     smem = pl.BlockSpec(memory_space=pltpu.SMEM)
     return pl.pallas_call(
@@ -190,19 +237,19 @@
             jax.ShapeDtypeStruct((2, rows, rows), F32),
             jax.ShapeDtypeStruct(probe.shape, F32),
             jax.ShapeDtypeStruct((slots, 2), F32),
-            jax.ShapeDtypeStruct((8, n), F32),
+            jax.ShapeDtypeStruct((8, 128), F32),
             jax.ShapeDtypeStruct((1,), F32),
         ),
         in_specs=[smem, smem, vmem, vmem, vmem, vmem, vmem],
         out_specs=(vmem, vmem, smem, vmem, smem),
         scratch_shapes=[
-            pltpu.VMEM((2, n + 8, 384), F32),
             pltpu.VMEM((2, n, n), F32),
             pltpu.VMEM((modes, 2, n, n), F32),
             pltpu.VMEM((n, n), F32),
             pltpu.VMEM((2, n, n), F32),
             pltpu.VMEM((n, n // 2), F32),
             pltpu.VMEM((n, n // 2), F32),
+            pltpu.VMEM((slots, 3, 8, 128), F32),
         ],
         compiler_params=pltpu.CompilerParams(vmem_limit_bytes=50 * 2**20),
     )(pos, count, canvas, probe, amp, jnp.asarray(dft_tables(n)), jnp.asarray(parity_table(n)))
@@ -303,7 +350,7 @@
     cells = obj.shape[1]
     return pl.pallas_call(
         functools.partial(halo_kernel, limits),
-        out_shape=jax.ShapeDtypeStruct((2, cells + 2 * HALO + 8, cells + 3 * HALO), F32),
+        out_shape=jax.ShapeDtypeStruct((2, cells + 2 * HALO, cells + 2 * HALO), F32),
         in_specs=[pl.BlockSpec(memory_space=pl.ANY)],
         out_specs=pl.BlockSpec(memory_space=pl.ANY),
         scratch_shapes=[
@@ -317,74 +364,58 @@
     )(obj)
 
 
+ORDERS = [(0, 1, 2), (1, 2, 0), (2, 0, 1), (1, 0, 2)]
+
+
+def spots():
+    row, col = place()
+    return (row // 2 % 2 * 2 + col // 4, row // 4, col % 4)
+
+
+def along(axis, by):
+    row, col = place()
+    at = list(spots())
+    at[axis] = (at[axis] + by) % 4
+    return (at[1] * 4 + at[0] // 2 * 2 + row % 2, at[0] % 2 * 4 + at[2])
+
+
 def finish_kernel(limits, spread_ref, pg_ref, energy_ref, obj_ref, probe_ref, illum_ref,
-                  onew_ref, pnew_ref, land_rows, land_cols, land_corners, mate_half, mate_energy, outbox, inbox,
-                  fold_send, fold_recv, mate_send, mate_recv, bulk):
+                  onew_ref, pnew_ref, land_rows, land_cols, land_corners, total_ref, mate_half, mate_energy, warm, heat,
+                  box1, box2, box3, fold_send, fold_recv, mate_send, mate_recv, down_send, down_recv, up_send, up_recv,
+                  heat_send, heat_recv):
     cells = obj_ref.shape[1]
     row, col = place()
     core = row % 2
     mate = (row + 1 - 2 * core, col)
-    pairs, cols = limits[0] // 2, limits[1]
-    chips = pairs * cols
-    me = row // 2 * cols + col
-    chunk = pg_ref.shape[1] // chips
-
-    def peer(d):
-        pair = (row // 2 + d // cols) % pairs
-        at = (col + d % cols) % cols
-        return pair * cols + at, (2 * pair + core, at)
+    at = spots()
+    units = len(ORDERS)
+    unit = pg_ref.shape[1] // units
 
     barrier, total = greet_sides(limits)
-
-    def greet(d, c):
-        pl.semaphore_signal(barrier, inc=1, device_id=peer(d)[1], device_id_type=MESH)
-        return c
-
     pl.semaphore_signal(barrier, inc=1, device_id=mate, device_id_type=MESH)
-    lax.fori_loop(1, chips, greet, 0)
-    pl.semaphore_wait(barrier, total + chips)
-
-    def to_mate(src, dst, i):
-        return pltpu.make_async_remote_copy(src_ref=src, dst_ref=dst, send_sem=mate_send.at[i], recv_sem=mate_recv.at[i],
-                                            device_id=mate, device_id_type=MESH)
-
-    first = to_mate(pg_ref.at[1 - core], mate_half, 0)
-    second = to_mate(energy_ref, mate_energy, 1)
-    first.start()
-    second.start()
-    first.wait()
-    second.wait()
-    warm = energy_ref[...] + mate_energy[...]
-
-    def pack(q, c):
-        rows = pl.ds(pl.multiple_of(q * chunk, chunk), chunk)
-        outbox[q, pl.ds(0, chunk), :] = pg_ref[core, rows, :] + mate_half[rows, :]
-        outbox[q, pl.ds(chunk, 8), :] = warm
-        return c
-
-    lax.fori_loop(0, chips, pack, 0)
-
-    def scatter(d, c):
-        q, device = peer(d)
-        pltpu.make_async_remote_copy(src_ref=outbox.at[q], dst_ref=inbox.at[d - 1], send_sem=bulk.at[0], recv_sem=bulk.at[1],
-                                     device_id=device, device_id_type=MESH).start()
-        return c
-
-    lax.fori_loop(1, chips, scatter, 0)
+    for axis in range(3):
+        for by in (1, 2, 3):
+            pl.semaphore_signal(barrier, inc=1, device_id=along(axis, by), device_id_type=MESH)
+    pl.semaphore_wait(barrier, total + 10)
+
+    def remote(src, dst, device, send, recv):
+        return pltpu.make_async_remote_copy(src_ref=src, dst_ref=dst, send_sem=send, recv_sem=recv,
+                                            device_id=device, device_id_type=MESH)
+
+    firsts = [remote(energy_ref, mate_energy, mate, mate_send.at[0], mate_recv.at[0])]
+    for u in range(units):
+        rows = pl.ds(u * unit, unit)
+        firsts.append(remote(pg_ref.at[1 - core, rows], mate_half.at[rows], mate, mate_send.at[1 + u], mate_recv.at[1 + u]))
+    for copy in firsts:
+        copy.start()
 
     folds = []
     for i, side in enumerate(SIDES):
         here = present(side, limits)
         back = SIDES.index((-side[0], -side[1]))
         land = land_rows.at[back] if i < 2 else land_cols.at[back - 2] if i < 4 else land_corners.at[back - 4]
-        send = pltpu.make_async_remote_copy(
-            src_ref=spread_ref.at[:, rim(side[0], cells), rim(side[1], cells)],
-            dst_ref=land,
-            send_sem=fold_send.at[i],
-            recv_sem=fold_recv.at[back],
-            device_id=neighbour(side),
-            device_id_type=MESH,
-        )
+        send = remote(spread_ref.at[:, rim(side[0], cells), rim(side[1], cells)], land, neighbour(side),
+                      fold_send.at[i], fold_recv.at[back])
         mine = land_rows.at[i] if i < 2 else land_cols.at[i - 2] if i < 4 else land_corners.at[i - 4]
         arrive = pltpu.make_async_copy(mine, mine, fold_recv.at[i])
         folds.append((here, send, arrive, side, mine))
@@ -393,20 +424,53 @@
         def _(send=send):
             send.start()
 
-    lower = inbox.at[pl.ds(0, chips - 1)]
-    pltpu.make_async_copy(lower, lower, bulk.at[0]).wait()
-    pltpu.make_async_copy(lower, lower, bulk.at[1]).wait()
-    summed = lax.fori_loop(0, chips - 1, lambda d, c: c + inbox[d], outbox[me])
-    here_rows = pl.ds(pl.multiple_of(me * chunk, chunk), chunk)
-    pnew_ref[core, here_rows, :] = probe_ref[core, here_rows, :] + summed[:chunk] / (summed[chunk:chunk + 1] + EPSILON)
-    out = pnew_ref.at[core, here_rows]
-
-    def gather(d, c):
-        pltpu.make_async_remote_copy(src_ref=out, dst_ref=out, send_sem=bulk.at[2], recv_sem=bulk.at[3],
-                                     device_id=peer(d)[1], device_id_type=MESH).start()
-        return c
-
-    lax.fori_loop(1, chips, gather, 0)
+    def piece(u, depth, spot):
+        order = ORDERS[u]
+        start = u * unit
+        if depth == 1:
+            return pl.ds(pl.multiple_of(start + spot * (unit // 4), unit // 4), unit // 4), slice(None)
+        start = start + at[order[0]] * (unit // 4)
+        if depth == 2:
+            return pl.ds(pl.multiple_of(start + spot * (unit // 16), unit // 16), unit // 16), slice(None)
+        start = start + at[order[1]] * (unit // 16)
+        return (pl.ds(pl.multiple_of(start + spot // 2 * 8, 8), 8), pl.ds(pl.multiple_of(spot % 2 * 128, 128), 128))
+
+    def own(u, depth):
+        return piece(u, depth, at[ORDERS[u][depth - 1]])
+
+    boxes = (box1, box2, box3)
+    waiting = []
+
+    def down(u, depth):
+        axis = ORDERS[u][depth - 1]
+        out = []
+        for by in (1, 2, 3):
+            copy = remote(total_ref.at[piece(u, depth, (at[axis] + by) % 4)], boxes[depth - 1].at[u, by - 1], along(axis, by),
+                          down_send.at[u, depth - 1, by - 1], down_recv.at[u, depth - 1, by - 1])
+            copy.start()
+            out.append(copy)
+        waiting.extend(out)
+        return out
+
+    def pass_heat(axis):
+        out = []
+        for by in (1, 2, 3):
+            copy = remote(warm.at[axis], heat.at[axis, by - 1], along(axis, by), heat_send.at[axis, by - 1], heat_recv.at[axis, by - 1])
+            copy.start()
+            out.append(copy)
+        waiting.extend(out)
+        return out
+
+    firsts[0].wait_recv()
+    warm[0] = energy_ref[...] + mate_energy[...]
+    hot = pass_heat(0)
+    flying = []
+    for u in range(units):
+        rows = pl.ds(u * unit, unit)
+        firsts[1 + u].wait_recv()
+        total_ref[rows, :] = pg_ref[core, rows, :] + mate_half[rows, :]
+        flying.append(down(u, 1))
+    waiting.extend(firsts)
 
     share = 1.0 / illum_ref[0]
     step_rows = 64
@@ -419,6 +483,56 @@
         return c
 
     lax.fori_loop(0, cells // step_rows, base, 0)
+
+    for depth in (1, 2, 3):
+        for copy in hot:
+            copy.wait_recv()
+        fresh = warm[depth - 1] + heat[depth - 1, 0] + heat[depth - 1, 1] + heat[depth - 1, 2]
+        if depth < 3:
+            warm[depth] = fresh
+            hot = pass_heat(depth)
+        for u in range(units):
+            for copy in flying[u]:
+                copy.wait_recv()
+            box = boxes[depth - 1]
+            where = own(u, depth)
+            summed = total_ref[where] + box[u, 0] + box[u, 1] + box[u, 2]
+            if depth < 3:
+                total_ref[where] = summed
+                flying[u] = down(u, depth + 1)
+            else:
+                pnew_ref[(core,) + where] = probe_ref[(core,) + where] + summed / (fresh[:, :128] + EPSILON)
+
+    def up(u, depth):
+        axis = ORDERS[u][depth - 1]
+        spot = pnew_ref.at[(core,) + own(u, depth)]
+        out = []
+        for by in (1, 2, 3):
+            landed = pnew_ref.at[(core,) + piece(u, depth, (at[axis] + 4 - by) % 4)]
+            copy = remote(spot, spot, along(axis, by), up_send.at[u, depth - 1, by - 1], up_recv.at[u, depth - 1, by - 1])
+            copy.start()
+            waiting.append(copy)
+            out.append(pltpu.make_async_copy(landed, landed, up_recv.at[u, depth - 1, by - 1]))
+        return out
+
+    for u in range(units):
+        flying[u] = up(u, 3)
+    lasts = []
+    for depth in (3, 2, 1):
+        for u in range(units):
+            for copy in flying[u]:
+                copy.wait()
+            if depth > 1:
+                flying[u] = up(u, depth - 1)
+            else:
+                rows = pl.ds(u * unit, unit)
+                done = pnew_ref.at[core, rows]
+                copy = remote(done, done, mate, mate_send.at[5 + u], mate_recv.at[5 + u])
+                copy.start()
+                waiting.append(copy)
+                got = pnew_ref.at[1 - core, rows]
+                lasts.append(pltpu.make_async_copy(got, got, mate_recv.at[5 + u]))
+
     for here, send, arrive, side, mine in folds:
         @pl.when(here)
         def _(send=send, arrive=arrive, side=side, mine=mine):
@@ -427,20 +541,19 @@
             for part in range(2):
                 onew_ref[part, edge(side[0], cells), edge(side[1], cells)] += mine[part] * share
 
-    rest = pnew_ref.at[core, pl.ds(0, (chips - 1) * chunk)]
-    pltpu.make_async_copy(rest, rest, bulk.at[2]).wait()
-    pltpu.make_async_copy(rest, rest, bulk.at[3]).wait()
-    last = to_mate(pnew_ref.at[core], pnew_ref.at[core], 2)
-    last.start()
-    last.wait()
+    for copy in lasts:
+        copy.wait()
+    for copy in waiting:
+        copy.wait_send()
 
 
 def finish(spread, pg, energy, obj, probe, illum, limits):
     cells = obj.shape[1]
     rows, lanes = probe.shape[1], probe.shape[2]
-    chips = limits[0] * limits[1] // 2
-    chunk = rows // chips
+    units = len(ORDERS)
+    unit = rows // units
     vmem = pl.BlockSpec(memory_space=pltpu.VMEM)
+    dma = pltpu.SemaphoreType.DMA
     return pl.pallas_call(
         functools.partial(finish_kernel, limits),
         out_shape=(jax.ShapeDtypeStruct(obj.shape, F32), jax.ShapeDtypeStruct(probe.shape, F32)),
@@ -451,14 +564,16 @@
             pltpu.VMEM((2, 2, cells, HALO), F32),
             pltpu.VMEM((4, 2, HALO, HALO), F32),
             pltpu.VMEM((rows, lanes), F32),
-            pltpu.VMEM((8, lanes), F32),
-            pltpu.VMEM((chips, chunk + 8, lanes), F32),
-            pltpu.VMEM((chips, chunk + 8, lanes), F32),
-            pltpu.SemaphoreType.DMA((8,)),
-            pltpu.SemaphoreType.DMA((8,)),
-            pltpu.SemaphoreType.DMA((3,)),
-            pltpu.SemaphoreType.DMA((3,)),
-            pltpu.SemaphoreType.DMA((4,)),
+            pltpu.VMEM((rows, lanes), F32),
+            pltpu.VMEM((8, 128), F32),
+            pltpu.VMEM((3, 8, 128), F32),
+            pltpu.VMEM((3, 3, 8, 128), F32),
+            pltpu.VMEM((units, 3, unit // 4, lanes), F32),
+            pltpu.VMEM((units, 3, unit // 16, lanes), F32),
+            pltpu.VMEM((units, 3, 8, 128), F32),
+            dma((8,)), dma((8,)), dma((9,)), dma((9,)),
+            dma((units, 3, 3)), dma((units, 3, 3)), dma((units, 3, 3)), dma((units, 3, 3)),
+            dma((3, 3)), dma((3, 3)),
         ],
         compiler_params=pltpu.CompilerParams(collective_id=1, has_side_effects=True, vmem_limit_bytes=40 * 2**20),
     )(spread, pg, energy, obj, probe, illum)

time: 203 us -> 167 us (0.82)
  Pallas kernels: 188 us -> 153 us
    pallas_call x1, Pallas kernels: 122 us -> 85.6 us  [finish(): pl.pallas_call(functools.partial(finish_kernel, limits), out_shape=(jax.S...]
where the time goes in v2:
time: 167 us
  Pallas kernels  153 us (92%)
  local copies, waits for them, and re-layouts  12.5 us (7%)
    pallas_call x1, Pallas kernels, finish(): pl.pallas_call(functools.partial(finish_kernel, limits), out_shape=(jax.S...  85.6 us
    pallas_call x1, Pallas kernels, step(): pl.pallas_call(step_kernel, out_shape=(jax.ShapeDtypeStruct((2, rows, row...  44.6 us
    pallas_call x1, Pallas kernels, exchange_halo(): pl.pallas_call(functools.partial(halo_kernel, limits), out_shape=jax.Shap...  22.6 us
    unnamed x20, local copies, waits for them, and re-layouts  11 us

profile of v2, /device:TPU:1, one launch (start us, length us, event | category | flops | bytes accessed | tf_op | source)
XLA Modules:
  0.0 166.6 jit_solution(6334968297148867220)
XLA Ops:
  1.3 0.8 copy.10.pos_ref
  2.0 0.0 copy-start.1
  2.0 1.6 copy-done.1
  3.6 0.0 copy-start.6
  3.6 0.0 copy-start.7
  3.6 0.0 copy-start.8
  3.6 22.6 %shard_map.94.canvas_ref = f32[2,768,768]{2,1,0:T(8,128)S(1)} custom-call(f32[2,512,512]{2,1,0:T(8,128)S(1)} %copy-done.1), custom_call_target="tpu_custom_call" | custom-call | tf_op jit(solution)/shard_map/pallas_call | solution.py:351
  26.3 0.0 copy-start
  26.3 2.1 %copy-done = f32[2,768,768]{2,1,0:T(8,128)} copy-done((f32[2,768,768]{2,1,0:T(8,128)}, f32[2,768,768]{2,1,0:T(8,128)S(1)}, u32[]{:S(2)}) %copy-start) | copy-done | bytes 4718616
  28.4 0.0 copy-done.6
  28.4 0.0 copy-done.7
  28.4 0.0 copy-done.8
  28.4 0.0 copy-start.2
  28.4 0.0 copy-start.3
  28.4 44.6 %shard_map.95 = (f32[2,768,768]{2,1,0:T(8,128)}, f32[2,4,256,256]{3,2,1,0:T(8,128)}, f32[6,2]{1,0:T(8,128)S(1)}, f32[8,128]{1,0:T(8,128)S(1)}, f32[1]{0:T(128)}) custom-call(s32[6,2]{1,0:T(8,128)S(1)} %copy.10.pos_ref, s32[1]{0:T(128)} %bitcast.7.count_ref, f32[2,768,768]{2,1,0:T(8,128)} %copy-done, f32[2,4,256,256]{3,2,1,0:T(8,128)} %probe_ref.1, ...), custom_call_target="tpu_custom_call" | custom-call | tf_op jit(solution)/shard_map/pallas_call | solution.py:234
  73.1 0.0 copy-done.2
  73.1 0.0 copy-done.3
  73.1 0.0 copy-start.4
  73.1 1.6 copy-done.4
  74.7 85.6 %shard_map.96 = (f32[2,512,512]{2,1,0:T(8,128)S(1)}, f32[2,1024,256]{2,1,0:T(8,128)S(1)}) custom-call(f32[2,768,768]{2,1,0:T(8,128)} %get-tuple-element.10.spread_ref, f32[2,1024,256]{2,1,0:T(8,128)S(1)} %bitcast.9, f32[8,128]{1,0:T(8,128)S(1)} %get-tuple-element.12.energy_ref, f32[2,512,512]{2,1,0:T(8,128)S(1)} %copy-done.2, f32[2,1024,256]{2,1,0:T(8,128)S(1)} %bitcast.8, ...), custom_call_target="tpu_custom_call" | custom-call | tf_op jit(solution)/shard_map/pallas_call | solution.py:557
  160.3 0.0 copy-start.5
  160.3 1.3 copy-done.5
  161.6 0.6 copy.11
  162.2 3.1 %copy.15 = f32[2,512,512]{2,1,0:T(8,128)} copy(f32[2,512,512]{2,1,0:T(8,128)} %copy-done.5) | data formatting | bytes 4194304
  165.3 1.3 copy.16
Async XLA Ops:
  2.0 1.6 copy-start.1
  3.6 24.8 %copy-start.6 = (f32[1,1,6,256,256]{4,3,2,1,0:T(8,128)S(1)}, f32[1,1,6,256,256]{4,3,2,1,0:T(8,128)}, u32[]{:S(2)}) copy-start(f32[1,1,6,256,256]{4,3,2,1,0:T(8,128)} %param.9) | copy-start | bytes 4718596
  3.6 24.8 %copy-start.7 = (bf16[4,2,256,256]{3,2,1,0:T(8,128)(2,1)S(1)}, bf16[4,2,256,256]{3,2,1,0:T(8,128)(2,1)}, u32[]{:S(2)}) copy-start(bf16[4,2,256,256]{3,2,1,0:T(8,128)(2,1)} %constant.4.clone.tab_ref) | copy-start | bytes 3145732
  3.6 24.8 %copy-start.8 = (bf16[256,256]{1,0:T(8,128)(2,1)S(1)}, bf16[256,256]{1,0:T(8,128)(2,1)}, u32[]{:S(2)}) copy-start(bf16[256,256]{1,0:T(8,128)(2,1)} %constant.5.clone.par_ref) | copy-start | bytes 393220
  26.3 2.1 %copy-start = (f32[2,768,768]{2,1,0:T(8,128)}, f32[2,768,768]{2,1,0:T(8,128)S(1)}, u32[]{:S(2)}) copy-start(f32[2,768,768]{2,1,0:T(8,128)S(1)} %shard_map.94.canvas_ref) | copy-start | bytes 14155780
  28.4 44.6 %copy-start.2 = (f32[2,512,512]{2,1,0:T(8,128)S(1)}, f32[2,512,512]{2,1,0:T(8,128)}, u32[]{:S(2)}) copy-start(f32[2,512,512]{2,1,0:T(8,128)} %obj_ref.3) | copy-start | bytes 6291460
  28.4 44.7 %copy-start.3 = (f32[2,4,256,256]{3,2,1,0:T(8,128)S(1)}, f32[2,4,256,256]{3,2,1,0:T(8,128)}, u32[]{:S(2)}) copy-start(f32[2,4,256,256]{3,2,1,0:T(8,128)} %probe_ref.1) | copy-start | bytes 6291460
  73.1 1.6 copy-start.4
  160.3 1.3 copy-start.5

commit v3 on v2

--- a/solution.py
+++ b/solution.py
@@ -256,11 +256,210 @@
 
 
 MESH = pl.DeviceIdType.MESH
-SIDES = [(-1, 0), (1, 0), (0, -1), (0, 1), (-1, -1), (-1, 1), (1, -1), (1, 1)]
 
 
 def place():
     return lax.axis_index("row"), lax.axis_index("col")
+
+
+def remote(src, dst, device, send, recv):
+    return pltpu.make_async_remote_copy(src_ref=src, dst_ref=dst, send_sem=send, recv_sem=recv,
+                                        device_id=device, device_id_type=MESH)
+
+
+def landed(ref, sem):
+    return pltpu.make_async_copy(ref, ref, sem)
+
+
+def roles(limits):
+    row, col = place()
+    rows, cols = limits
+    core = row % 2
+    seam = cols // 2
+    up, down = row > 0, row < rows - 1
+    outer = jnp.where(core == 0, row - 1, row + 1)
+    has_outer = jnp.logical_and(outer >= 0, outer < rows)
+    near = {-1: jnp.logical_and(col > 0, col != seam), 1: jnp.logical_and(col < cols - 1, col != seam - 1)}
+    at_seam = {-1: col == seam, 1: col == seam - 1}
+    has = {-1: col > 0, 1: col < cols - 1}
+    relay = {0: col == cols - 1, 1: col == 0}
+    return dict(row=row, col=col, core=core, mate=(row + 1 - 2 * core, col), outer=(outer, col), has_outer=has_outer,
+                near=near, at_seam=at_seam, has=has, relay=relay, seam=seam, cols=cols)
+
+
+def greet(r):
+    barrier = pltpu.get_barrier_semaphore()
+    row, col, cols, seam = r["row"], r["col"], r["cols"], r["seam"]
+    seam_any = jnp.logical_or(r["at_seam"][-1], r["at_seam"][1])
+    relay_any = jnp.logical_or(r["relay"][0], r["relay"][1])
+    pl.semaphore_signal(barrier, inc=1, device_id=r["mate"], device_id_type=MESH)
+    total = jnp.int32(1)
+
+    def to(cond, device):
+        @pl.when(cond)
+        def _():
+            pl.semaphore_signal(barrier, inc=1, device_id=device, device_id_type=MESH)
+
+        return cond.astype(jnp.int32)
+
+    total += to(r["has_outer"], r["outer"])
+    for dc in (-1, 1):
+        total += to(r["has"][dc], (row, col + dc))
+    for target in (0, cols - 1):
+        total += to(seam_any, (row, target))
+    for target in (seam - 1, seam):
+        total += to(relay_any, (row, target))
+    return barrier, total
+
+
+def when(cond, *actions):
+    @pl.when(cond)
+    def _():
+        for action in actions:
+            action()
+
+
+def halo_kernel(limits, obj_ref, canvas_ref, zeros, passing, own_sem, zero_sems, row_send, row_recv, col_send, col_recv,
+                seam_send, seam_recv, pass_send, pass_recv, corner_send, corner_recv):
+    cells = obj_ref.shape[1]
+    half = cells // 2
+    r = roles(limits)
+    row, col, core, seam, cols = r["row"], r["col"], r["core"], r["seam"], r["cols"]
+    barrier, total = greet(r)
+    own = pltpu.make_async_copy(obj_ref, canvas_ref.at[:, pl.ds(HALO, cells), pl.ds(HALO, cells)], own_sem)
+    own.start()
+    zeros[...] = jnp.zeros_like(zeros)
+    pl.semaphore_wait(barrier, total)
+
+    outer_from = pl.multiple_of(jnp.where(core == 0, 0, cells - HALO), HALO)
+    inner_from = pl.multiple_of(jnp.where(core == 0, cells - HALO, 0), HALO)
+    outer_at = pl.multiple_of(jnp.where(core == 0, 0, cells + HALO), HALO)
+    inner_at = pl.multiple_of(jnp.where(core == 0, cells + HALO, 0), HALO)
+    strips = ((0, HALO), (cells - HALO, HALO), (HALO, cells - 2 * HALO))
+    edge_from = {-1: 0, 1: cells - HALO}
+    rim_at = {-1: 0, 1: cells + HALO}
+    side = {-1: 0, 1: 1}
+
+    def canvas(top, tall, left, wide):
+        return canvas_ref.at[:, pl.ds(top, tall), pl.ds(left, wide)]
+
+    def tile(top, tall, left, wide):
+        return obj_ref.at[:, pl.ds(top, tall), pl.ds(left, wide)]
+
+    edges = {}
+    seams = {}
+    for dc in (-1, 1):
+        edges[dc] = remote(tile(0, cells, edge_from[dc], HALO), canvas(HALO, cells, rim_at[-dc], HALO), (row, col + dc),
+                           col_send.at[side[dc]], col_recv.at[side[-dc]])
+        when(r["near"][dc], edges[dc].start)
+        pair = []
+        for part, target in ((0, cols - 1), (1, 0)):
+            pair.append(remote(tile(part * half, half, edge_from[dc], HALO), passing.at[side[dc]], (row, target),
+                               seam_send.at[part], seam_recv.at[side[dc]]))
+        seams[dc] = pair
+        when(r["at_seam"][dc], pair[0].start, pair[1].start)
+
+    inner = remote(tile(inner_from, HALO, 0, cells), canvas(outer_at_of_mate(inner_at, cells), HALO, HALO, cells), r["mate"],
+                   row_send.at[3], row_recv.at[3])
+    inner.start()
+    outers = []
+    for i, (left, wide) in enumerate(strips):
+        copy = remote(tile(outer_from, HALO, left, wide), canvas(outer_at_of_mate(outer_at, cells), HALO, HALO + left, wide), r["outer"],
+                      row_send.at[i], row_recv.at[i])
+        outers.append(copy)
+        when(r["has_outer"], copy.start)
+    blanks = []
+    for i, (cond, ref) in enumerate((
+        (jnp.logical_not(r["has_outer"]), canvas(outer_at, HALO, 0, cells + 2 * HALO)),
+        (jnp.logical_not(r["has"][-1]), canvas(HALO, cells, 0, HALO)),
+        (jnp.logical_not(r["has"][1]), canvas(HALO, cells, cells + HALO, HALO)),
+    )):
+        source = zeros.at[:, pl.ds(0, HALO), :] if i == 0 else zeros.at[:, pl.ds(0, cells), pl.ds(0, HALO)]
+        copy = pltpu.make_async_copy(source, ref, zero_sems.at[i])
+        blanks.append((cond, copy))
+        when(cond, copy.start)
+    for dc in (-1, 1):
+        for k, top in ((0, inner_at), (1, outer_at)):
+            need = jnp.logical_not(r["has"][dc])
+            if k:
+                need = jnp.logical_and(need, r["has_outer"])
+            copy = pltpu.make_async_copy(zeros.at[:, pl.ds(0, HALO), pl.ds(0, HALO)], canvas(top, HALO, rim_at[dc], HALO),
+                                         zero_sems.at[3 + 2 * side[dc] + k])
+            blanks.append((need, copy))
+            when(need, copy.start)
+
+    def forward(part, dc):
+        target = seam if dc == 1 else seam - 1
+        return remote(passing.at[side[dc]], canvas(HALO + part * half, half, rim_at[-dc], HALO), (row, target),
+                      pass_send.at[side[dc]], pass_recv.at[part])
+
+    def relay(part, dc):
+        when(r["relay"][part], landed(passing.at[side[dc]], seam_recv.at[side[dc]]).wait, forward(part, dc).start)
+
+    relay(0, -1)
+    relay(1, 1)
+    corners = {}
+    for dc in (-1, 1):
+        i = side[dc]
+        strip = canvas(outer_at, HALO, HALO + edge_from[dc], HALO)
+        give = jnp.logical_and(r["has_outer"], r["has"][dc])
+        corners[dc] = (give, remote(strip, canvas(outer_at, HALO, rim_at[-dc], HALO), (row, col + dc),
+                                    corner_send.at[i], corner_recv.at[1 - i]))
+        when(r["has_outer"], landed(strip, row_recv.at[i]).wait)
+        when(give, corners[dc][1].start)
+    relay(0, 1)
+    relay(1, -1)
+    inside = {}
+    for dc in (-1, 1):
+        i = side[dc]
+        near_mate = pl.multiple_of(inner_from + HALO, HALO)
+        when(r["near"][dc], landed(canvas(HALO, cells, rim_at[dc], HALO), col_recv.at[i]).wait)
+        for part in range(2):
+            when(r["at_seam"][dc], landed(canvas(HALO + part * half, half, rim_at[dc], HALO), pass_recv.at[part]).wait)
+        inside[dc] = remote(canvas(near_mate, HALO, rim_at[dc], HALO), canvas(outer_at_of_mate(inner_at, cells), HALO, rim_at[dc], HALO),
+                            r["mate"], corner_send.at[2 + i], corner_recv.at[2 + i])
+        when(r["has"][dc], inside[dc].start)
+
+    inner.wait_send()
+    landed(canvas(inner_at, HALO, HALO, cells), row_recv.at[3]).wait()
+    when(r["has_outer"], *[copy.wait_send for copy in outers])
+    when(r["has_outer"], landed(canvas(outer_at, HALO, HALO + strips[2][0], strips[2][1]), row_recv.at[2]).wait)
+    for dc in (-1, 1):
+        i = side[dc]
+        when(r["near"][dc], edges[dc].wait_send)
+        when(r["at_seam"][dc], seams[dc][0].wait_send, seams[dc][1].wait_send)
+        for part in range(2):
+            when(r["relay"][part], forward(part, dc).wait_send)
+        when(corners[dc][0], corners[dc][1].wait_send, landed(canvas(outer_at, HALO, rim_at[dc], HALO), corner_recv.at[i]).wait)
+        when(r["has"][dc], inside[dc].wait_send, landed(canvas(inner_at, HALO, rim_at[dc], HALO), corner_recv.at[2 + i]).wait)
+    for cond, copy in blanks:
+        when(cond, copy.wait)
+    own.wait()
+
+
+def outer_at_of_mate(at, cells):
+    return pl.multiple_of(cells + HALO - at, HALO)
+
+
+def exchange_halo(obj, limits):
+    cells = obj.shape[1]
+    dma = pltpu.SemaphoreType.DMA
+    return pl.pallas_call(
+        functools.partial(halo_kernel, limits),
+        out_shape=jax.ShapeDtypeStruct((2, cells + 2 * HALO, cells + 2 * HALO), F32),
+        in_specs=[pl.BlockSpec(memory_space=pl.ANY)],
+        out_specs=pl.BlockSpec(memory_space=pl.ANY),
+        scratch_shapes=[
+            pltpu.VMEM((2, cells, cells + 2 * HALO), F32),
+            pltpu.VMEM((2, 2, cells // 2, HALO), F32),
+            dma, dma((7,)), dma((4,)), dma((4,)), dma((2,)), dma((2,)), dma((2,)), dma((2,)), dma((2,)), dma((2,)),
+            dma((4,)), dma((4,)),
+        ],
+        compiler_params=pltpu.CompilerParams(collective_id=0, has_side_effects=True, vmem_limit_bytes=16 * 2**20),
+    )(obj)
+
+
+SIDES = [(-1, 0), (1, 0), (0, -1), (0, 1), (-1, -1), (-1, 1), (1, -1), (1, 1)]
 
 
 def present(side, limits):
@@ -298,70 +497,6 @@
             pl.semaphore_signal(barrier, inc=1, device_id=neighbour(side), device_id_type=MESH)
 
     return barrier, total
-
-
-def halo_kernel(limits, obj_ref, canvas_ref, zeros, own_sem, zero_sems, send_sems, recv_sems):
-    cells = obj_ref.shape[1]
-    barrier, total = greet_sides(limits)
-    own = pltpu.make_async_copy(obj_ref, canvas_ref.at[:, pl.ds(HALO, cells), pl.ds(HALO, cells)], own_sem)
-    own.start()
-    zeros[...] = jnp.zeros_like(zeros)
-    pl.semaphore_wait(barrier, total)
-    steps = []
-    for i, side in enumerate(SIDES):
-        here = present(side, limits)
-        back = SIDES.index((-side[0], -side[1]))
-        send = pltpu.make_async_remote_copy(
-            src_ref=obj_ref.at[:, edge(side[0], cells), edge(side[1], cells)],
-            dst_ref=canvas_ref.at[:, rim(-side[0], cells), rim(-side[1], cells)],
-            send_sem=send_sems.at[i],
-            recv_sem=recv_sems.at[back],
-            device_id=neighbour(side),
-            device_id_type=MESH,
-        )
-        landed = canvas_ref.at[:, rim(side[0], cells), rim(side[1], cells)]
-        tall, wide = (cells if side[0] == 0 else HALO), (cells if side[1] == 0 else HALO)
-        blank = pltpu.make_async_copy(zeros.at[:, pl.ds(0, tall), pl.ds(0, wide)], landed, zero_sems.at[i])
-        arrive = pltpu.make_async_copy(landed, landed, recv_sems.at[i])
-        steps.append((here, send, blank, arrive))
-
-        @pl.when(here)
-        def _(send=send):
-            send.start()
-
-        @pl.when(jnp.logical_not(here))
-        def _(blank=blank):
-            blank.start()
-
-    for here, send, blank, arrive in steps:
-        @pl.when(here)
-        def _(send=send, arrive=arrive):
-            send.wait_send()
-            arrive.wait()
-
-        @pl.when(jnp.logical_not(here))
-        def _(blank=blank):
-            blank.wait()
-
-    own.wait()
-
-
-def exchange_halo(obj, limits):
-    cells = obj.shape[1]
-    return pl.pallas_call(
-        functools.partial(halo_kernel, limits),
-        out_shape=jax.ShapeDtypeStruct((2, cells + 2 * HALO, cells + 2 * HALO), F32),
-        in_specs=[pl.BlockSpec(memory_space=pl.ANY)],
-        out_specs=pl.BlockSpec(memory_space=pl.ANY),
-        scratch_shapes=[
-            pltpu.VMEM((2, cells, cells), F32),
-            pltpu.SemaphoreType.DMA,
-            pltpu.SemaphoreType.DMA((8,)),
-            pltpu.SemaphoreType.DMA((8,)),
-            pltpu.SemaphoreType.DMA((8,)),
-        ],
-        compiler_params=pltpu.CompilerParams(collective_id=0, has_side_effects=True, vmem_limit_bytes=16 * 2**20),
-    )(obj)
 
 
 ORDERS = [(0, 1, 2), (1, 2, 0), (2, 0, 1), (1, 0, 2)]

time: 167 us -> 155 us (0.928)
  Pallas kernels: 153 us -> 141 us
    pallas_call x1, Pallas kernels: 85.6 us -> 74.2 us  [finish(): pl.pallas_call(functools.partial(finish_kernel, limits), out_shape=(jax.S...]
where the time goes in v3:
time: 155 us
  Pallas kernels  141 us (91%)
  local copies, waits for them, and re-layouts  12.5 us (8%)
    pallas_call x1, Pallas kernels, finish(): pl.pallas_call(functools.partial(finish_kernel, limits), out_shape=(jax.S...  74.2 us
    pallas_call x1, Pallas kernels, step(): pl.pallas_call(step_kernel, out_shape=(jax.ShapeDtypeStruct((2, rows, row...  44.6 us
    pallas_call x1, Pallas kernels, exchange_halo(): pl.pallas_call(functools.partial(halo_kernel, limits), out_shape=jax.Shap...  22.2 us
    unnamed x20, local copies, waits for them, and re-layouts  11 us

profile of v3, /device:TPU:1, one launch (start us, length us, event | category | flops | bytes accessed | tf_op | source)
XLA Modules:
  0.0 154.9 jit_solution(16692209967071865906)
XLA Ops:
  1.3 0.8 copy.10.pos_ref
  2.0 0.0 copy-start.1
  2.0 1.6 %copy-done.1 = f32[2,512,512]{2,1,0:T(8,128)S(1)} copy-done((f32[2,512,512]{2,1,0:T(8,128)S(1)}, f32[2,512,512]{2,1,0:T(8,128)}, u32[]{:S(2)}) %copy-start.1) | copy-done | bytes 2097176
  3.6 0.0 copy-start.6
  3.6 0.0 copy-start.7
  3.6 0.0 copy-start.8
  3.6 22.2 %shard_map.94.canvas_ref = f32[2,768,768]{2,1,0:T(8,128)S(1)} custom-call(f32[2,512,512]{2,1,0:T(8,128)S(1)} %copy-done.1), custom_call_target="tpu_custom_call" | custom-call | tf_op jit(solution)/shard_map/pallas_call | solution.py:447
  25.9 0.0 copy-start
  25.9 2.1 %copy-done = f32[2,768,768]{2,1,0:T(8,128)} copy-done((f32[2,768,768]{2,1,0:T(8,128)}, f32[2,768,768]{2,1,0:T(8,128)S(1)}, u32[]{:S(2)}) %copy-start) | copy-done | bytes 4718616
  28.0 0.0 copy-done.6
  28.0 0.0 copy-done.7
  28.0 0.0 copy-done.8
  28.0 0.0 copy-start.2
  28.1 0.0 copy-start.3
  28.1 44.6 %shard_map.95 = (f32[2,768,768]{2,1,0:T(8,128)}, f32[2,4,256,256]{3,2,1,0:T(8,128)}, f32[6,2]{1,0:T(8,128)S(1)}, f32[8,128]{1,0:T(8,128)S(1)}, f32[1]{0:T(128)}) custom-call(s32[6,2]{1,0:T(8,128)S(1)} %copy.10.pos_ref, s32[1]{0:T(128)} %bitcast.7.count_ref, f32[2,768,768]{2,1,0:T(8,128)} %copy-done, f32[2,4,256,256]{3,2,1,0:T(8,128)} %probe_ref.1, ...), custom_call_target="tpu_custom_call" | custom-call | tf_op jit(solution)/shard_map/pallas_call | solution.py:234
  72.7 0.0 copy-done.2
  72.7 0.0 copy-done.3
  72.7 0.0 copy-start.4
  72.7 1.6 %copy-done.4 = f32[2,4,256,256]{3,2,1,0:T(8,128)S(1)} copy-done((f32[2,4,256,256]{3,2,1,0:T(8,128)S(1)}, f32[2,4,256,256]{3,2,1,0:T(8,128)}, u32[]{:S(2)}) %copy-start.4) | copy-done | bytes 2097176
  74.3 74.2 %shard_map.96 = (f32[2,512,512]{2,1,0:T(8,128)S(1)}, f32[2,1024,256]{2,1,0:T(8,128)S(1)}) custom-call(f32[2,768,768]{2,1,0:T(8,128)} %get-tuple-element.10.spread_ref, f32[2,1024,256]{2,1,0:T(8,128)S(1)} %bitcast.9, f32[8,128]{1,0:T(8,128)S(1)} %get-tuple-element.12.energy_ref, f32[2,512,512]{2,1,0:T(8,128)S(1)} %copy-done.2, f32[2,1024,256]{2,1,0:T(8,128)S(1)} %bitcast.8, ...), custom_call_target="tpu_custom_call" | custom-call | tf_op jit(solution)/shard_map/pallas_call | solution.py:692
  148.5 0.0 copy-start.5
  148.6 1.3 copy-done.5
  149.9 0.6 copy.11
  150.5 3.1 %copy.15 = f32[2,512,512]{2,1,0:T(8,128)} copy(f32[2,512,512]{2,1,0:T(8,128)} %copy-done.5) | data formatting | bytes 4194304
  153.6 1.3 copy.16
Async XLA Ops:
  2.0 1.6 %copy-start.1 = (f32[2,512,512]{2,1,0:T(8,128)S(1)}, f32[2,512,512]{2,1,0:T(8,128)}, u32[]{:S(2)}) copy-start(f32[2,512,512]{2,1,0:T(8,128)} %obj_ref.3) | copy-start | bytes 6291460
  3.6 24.4 %copy-start.6 = (f32[1,1,6,256,256]{4,3,2,1,0:T(8,128)S(1)}, f32[1,1,6,256,256]{4,3,2,1,0:T(8,128)}, u32[]{:S(2)}) copy-start(f32[1,1,6,256,256]{4,3,2,1,0:T(8,128)} %param.9) | copy-start | bytes 4718596
  3.6 24.4 %copy-start.7 = (bf16[4,2,256,256]{3,2,1,0:T(8,128)(2,1)S(1)}, bf16[4,2,256,256]{3,2,1,0:T(8,128)(2,1)}, u32[]{:S(2)}) copy-start(bf16[4,2,256,256]{3,2,1,0:T(8,128)(2,1)} %constant.4.clone.tab_ref) | copy-start | bytes 3145732
  3.6 24.4 %copy-start.8 = (bf16[256,256]{1,0:T(8,128)(2,1)S(1)}, bf16[256,256]{1,0:T(8,128)(2,1)}, u32[]{:S(2)}) copy-start(bf16[256,256]{1,0:T(8,128)(2,1)} %constant.5.clone.par_ref) | copy-start | bytes 393220
  25.9 2.1 %copy-start = (f32[2,768,768]{2,1,0:T(8,128)}, f32[2,768,768]{2,1,0:T(8,128)S(1)}, u32[]{:S(2)}) copy-start(f32[2,768,768]{2,1,0:T(8,128)S(1)} %shard_map.94.canvas_ref) | copy-start | bytes 14155780
  28.0 44.7 %copy-start.2 = (f32[2,512,512]{2,1,0:T(8,128)S(1)}, f32[2,512,512]{2,1,0:T(8,128)}, u32[]{:S(2)}) copy-start(f32[2,512,512]{2,1,0:T(8,128)} %obj_ref.3) | copy-start | bytes 6291460
  28.1 44.7 %copy-start.3 = (f32[2,4,256,256]{3,2,1,0:T(8,128)S(1)}, f32[2,4,256,256]{3,2,1,0:T(8,128)}, u32[]{:S(2)}) copy-start(f32[2,4,256,256]{3,2,1,0:T(8,128)} %probe_ref.1) | copy-start | bytes 6291460
  72.7 1.6 %copy-start.4 = (f32[2,4,256,256]{3,2,1,0:T(8,128)S(1)}, f32[2,4,256,256]{3,2,1,0:T(8,128)}, u32[]{:S(2)}) copy-start(f32[2,4,256,256]{3,2,1,0:T(8,128)} %get-tuple-element.11) | copy-start | bytes 6291460
  148.5 1.3 copy-start.5

commit v4 on v3

--- a/solution.py
+++ b/solution.py
@@ -459,44 +459,208 @@
     )(obj)
 
 
+def place():
+    return lax.axis_index("row"), lax.axis_index("col")
+
+
+def remote(src, dst, device, send, recv):
+    return pltpu.make_async_remote_copy(src_ref=src, dst_ref=dst, send_sem=send, recv_sem=recv,
+                                        device_id=device, device_id_type=MESH)
+
+
+def landed(ref, sem):
+    return pltpu.make_async_copy(ref, ref, sem)
+
+
+def roles(limits):
+    row, col = place()
+    rows, cols = limits
+    core = row % 2
+    seam = cols // 2
+    up, down = row > 0, row < rows - 1
+    outer = jnp.where(core == 0, row - 1, row + 1)
+    has_outer = jnp.logical_and(outer >= 0, outer < rows)
+    near = {-1: jnp.logical_and(col > 0, col != seam), 1: jnp.logical_and(col < cols - 1, col != seam - 1)}
+    at_seam = {-1: col == seam, 1: col == seam - 1}
+    has = {-1: col > 0, 1: col < cols - 1}
+    relay = {0: col == cols - 1, 1: col == 0}
+    return dict(row=row, col=col, core=core, mate=(row + 1 - 2 * core, col), outer=(outer, col), has_outer=has_outer,
+                near=near, at_seam=at_seam, has=has, relay=relay, seam=seam, cols=cols)
+
+
+def greet(r):
+    barrier = pltpu.get_barrier_semaphore()
+    row, col, cols, seam = r["row"], r["col"], r["cols"], r["seam"]
+    seam_any = jnp.logical_or(r["at_seam"][-1], r["at_seam"][1])
+    relay_any = jnp.logical_or(r["relay"][0], r["relay"][1])
+    pl.semaphore_signal(barrier, inc=1, device_id=r["mate"], device_id_type=MESH)
+    total = jnp.int32(1)
+
+    def to(cond, device):
+        @pl.when(cond)
+        def _():
+            pl.semaphore_signal(barrier, inc=1, device_id=device, device_id_type=MESH)
+
+        return cond.astype(jnp.int32)
+
+    total += to(r["has_outer"], r["outer"])
+    for dc in (-1, 1):
+        total += to(r["has"][dc], (row, col + dc))
+    for target in (0, cols - 1):
+        total += to(seam_any, (row, target))
+    for target in (seam - 1, seam):
+        total += to(relay_any, (row, target))
+    return barrier, total
+
+
+def when(cond, *actions):
+    @pl.when(cond)
+    def _():
+        for action in actions:
+            action()
+
+
+def halo_kernel(limits, obj_ref, canvas_ref, zeros, passing, own_sem, zero_sems, row_send, row_recv, col_send, col_recv,
+                seam_send, seam_recv, pass_send, pass_recv, corner_send, corner_recv):
+    cells = obj_ref.shape[1]
+    half = cells // 2
+    r = roles(limits)
+    row, col, core, seam, cols = r["row"], r["col"], r["core"], r["seam"], r["cols"]
+    barrier, total = greet(r)
+    own = pltpu.make_async_copy(obj_ref, canvas_ref.at[:, pl.ds(HALO, cells), pl.ds(HALO, cells)], own_sem)
+    own.start()
+    zeros[...] = jnp.zeros_like(zeros)
+    pl.semaphore_wait(barrier, total)
+
+    outer_from = pl.multiple_of(jnp.where(core == 0, 0, cells - HALO), HALO)
+    inner_from = pl.multiple_of(jnp.where(core == 0, cells - HALO, 0), HALO)
+    outer_at = pl.multiple_of(jnp.where(core == 0, 0, cells + HALO), HALO)
+    inner_at = pl.multiple_of(jnp.where(core == 0, cells + HALO, 0), HALO)
+    strips = ((0, HALO), (cells - HALO, HALO), (HALO, cells - 2 * HALO))
+    edge_from = {-1: 0, 1: cells - HALO}
+    rim_at = {-1: 0, 1: cells + HALO}
+    side = {-1: 0, 1: 1}
+
+    def canvas(top, tall, left, wide):
+        return canvas_ref.at[:, pl.ds(top, tall), pl.ds(left, wide)]
+
+    def tile(top, tall, left, wide):
+        return obj_ref.at[:, pl.ds(top, tall), pl.ds(left, wide)]
+
+    edges = {}
+    seams = {}
+    for dc in (-1, 1):
+        edges[dc] = remote(tile(0, cells, edge_from[dc], HALO), canvas(HALO, cells, rim_at[-dc], HALO), (row, col + dc),
+                           col_send.at[side[dc]], col_recv.at[side[-dc]])
+        when(r["near"][dc], edges[dc].start)
+        pair = []
+        for part, target in ((0, cols - 1), (1, 0)):
+            pair.append(remote(tile(part * half, half, edge_from[dc], HALO), passing.at[side[dc]], (row, target),
+                               seam_send.at[part], seam_recv.at[side[dc]]))
+        seams[dc] = pair
+        when(r["at_seam"][dc], pair[0].start, pair[1].start)
+
+    inner = remote(tile(inner_from, HALO, 0, cells), canvas(outer_at_of_mate(inner_at, cells), HALO, HALO, cells), r["mate"],
+                   row_send.at[3], row_recv.at[3])
+    inner.start()
+    outers = []
+    for i, (left, wide) in enumerate(strips):
+        copy = remote(tile(outer_from, HALO, left, wide), canvas(outer_at_of_mate(outer_at, cells), HALO, HALO + left, wide), r["outer"],
+                      row_send.at[i], row_recv.at[i])
+        outers.append(copy)
+        when(r["has_outer"], copy.start)
+    blanks = []
+    for i, (cond, ref) in enumerate((
+        (jnp.logical_not(r["has_outer"]), canvas(outer_at, HALO, 0, cells + 2 * HALO)),
+        (jnp.logical_not(r["has"][-1]), canvas(HALO, cells, 0, HALO)),
+        (jnp.logical_not(r["has"][1]), canvas(HALO, cells, cells + HALO, HALO)),
+    )):
+        source = zeros.at[:, pl.ds(0, HALO), :] if i == 0 else zeros.at[:, pl.ds(0, cells), pl.ds(0, HALO)]
+        copy = pltpu.make_async_copy(source, ref, zero_sems.at[i])
+        blanks.append((cond, copy))
+        when(cond, copy.start)
+    for dc in (-1, 1):
+        for k, top in ((0, inner_at), (1, outer_at)):
+            need = jnp.logical_not(r["has"][dc])
+            if k:
+                need = jnp.logical_and(need, r["has_outer"])
+            copy = pltpu.make_async_copy(zeros.at[:, pl.ds(0, HALO), pl.ds(0, HALO)], canvas(top, HALO, rim_at[dc], HALO),
+                                         zero_sems.at[3 + 2 * side[dc] + k])
+            blanks.append((need, copy))
+            when(need, copy.start)
+
+    def forward(part, dc):
+        target = seam if dc == 1 else seam - 1
+        return remote(passing.at[side[dc]], canvas(HALO + part * half, half, rim_at[-dc], HALO), (row, target),
+                      pass_send.at[side[dc]], pass_recv.at[part])
+
+    def relay(part, dc):
+        when(r["relay"][part], landed(passing.at[side[dc]], seam_recv.at[side[dc]]).wait, forward(part, dc).start)
+
+    relay(0, -1)
+    relay(1, 1)
+    corners = {}
+    for dc in (-1, 1):
+        i = side[dc]
+        strip = canvas(outer_at, HALO, HALO + edge_from[dc], HALO)
+        give = jnp.logical_and(r["has_outer"], r["has"][dc])
+        corners[dc] = (give, remote(strip, canvas(outer_at, HALO, rim_at[-dc], HALO), (row, col + dc),
+                                    corner_send.at[i], corner_recv.at[1 - i]))
+        when(r["has_outer"], landed(strip, row_recv.at[i]).wait)
+        when(give, corners[dc][1].start)
+    relay(0, 1)
+    relay(1, -1)
+    inside = {}
+    for dc in (-1, 1):
+        i = side[dc]
+        near_mate = pl.multiple_of(inner_from + HALO, HALO)
+        when(r["near"][dc], landed(canvas(HALO, cells, rim_at[dc], HALO), col_recv.at[i]).wait)
+        for part in range(2):
+            when(r["at_seam"][dc], landed(canvas(HALO + part * half, half, rim_at[dc], HALO), pass_recv.at[part]).wait)
+        inside[dc] = remote(canvas(near_mate, HALO, rim_at[dc], HALO), canvas(outer_at_of_mate(inner_at, cells), HALO, rim_at[dc], HALO),
+                            r["mate"], corner_send.at[2 + i], corner_recv.at[2 + i])
+        when(r["has"][dc], inside[dc].start)
+
+    inner.wait_send()
+    landed(canvas(inner_at, HALO, HALO, cells), row_recv.at[3]).wait()
+    when(r["has_outer"], *[copy.wait_send for copy in outers])
+    when(r["has_outer"], landed(canvas(outer_at, HALO, HALO + strips[2][0], strips[2][1]), row_recv.at[2]).wait)
+    for dc in (-1, 1):
+        i = side[dc]
+        when(r["near"][dc], edges[dc].wait_send)
+        when(r["at_seam"][dc], seams[dc][0].wait_send, seams[dc][1].wait_send)
+        for part in range(2):
+            when(r["relay"][part], forward(part, dc).wait_send)
+        when(corners[dc][0], corners[dc][1].wait_send, landed(canvas(outer_at, HALO, rim_at[dc], HALO), corner_recv.at[i]).wait)
+        when(r["has"][dc], inside[dc].wait_send, landed(canvas(inner_at, HALO, rim_at[dc], HALO), corner_recv.at[2 + i]).wait)
+    for cond, copy in blanks:
+        when(cond, copy.wait)
+    own.wait()
+
+
+def outer_at_of_mate(at, cells):
+    return pl.multiple_of(cells + HALO - at, HALO)
+
+
+def exchange_halo(obj, limits):
+    cells = obj.shape[1]
+    dma = pltpu.SemaphoreType.DMA
+    return pl.pallas_call(
+        functools.partial(halo_kernel, limits),
+        out_shape=jax.ShapeDtypeStruct((2, cells + 2 * HALO, cells + 2 * HALO), F32),
+        in_specs=[pl.BlockSpec(memory_space=pl.ANY)],
+        out_specs=pl.BlockSpec(memory_space=pl.ANY),
+        scratch_shapes=[
+            pltpu.VMEM((2, cells, cells + 2 * HALO), F32),
+            pltpu.VMEM((2, 2, cells // 2, HALO), F32),
+            dma, dma((7,)), dma((4,)), dma((4,)), dma((2,)), dma((2,)), dma((2,)), dma((2,)), dma((2,)), dma((2,)),
+            dma((4,)), dma((4,)),
+        ],
+        compiler_params=pltpu.CompilerParams(collective_id=0, has_side_effects=True, vmem_limit_bytes=16 * 2**20),
+    )(obj)
+
+
 SIDES = [(-1, 0), (1, 0), (0, -1), (0, 1), (-1, -1), (-1, 1), (1, -1), (1, 1)]
-
-
-def present(side, limits):
-    row, col = place()
-    fits = None
-    for at, by, limit in ((row, side[0], limits[0]), (col, side[1], limits[1])):
-        if by:
-            ok = at > 0 if by < 0 else at < limit - 1
-            fits = ok if fits is None else jnp.logical_and(fits, ok)
-    return fits
-
-
-def neighbour(side):
-    row, col = place()
-    return (row + side[0], col + side[1])
-
-
-def edge(by, cells):
-    return pl.ds(0, cells) if by == 0 else (pl.ds(0, HALO) if by < 0 else pl.ds(cells - HALO, HALO))
-
-
-def rim(by, cells):
-    return pl.ds(HALO, cells) if by == 0 else (pl.ds(0, HALO) if by < 0 else pl.ds(cells + HALO, HALO))
-
-
-def greet_sides(limits):
-    barrier = pltpu.get_barrier_semaphore()
-    total = jnp.int32(0)
-    for side in SIDES:
-        here = present(side, limits)
-        total += here.astype(jnp.int32)
-
-        @pl.when(here)
-        def _():
-            pl.semaphore_signal(barrier, inc=1, device_id=neighbour(side), device_id_type=MESH)
-
-    return barrier, total
 
 
 ORDERS = [(0, 1, 2), (1, 2, 0), (2, 0, 1), (1, 0, 2)]
@@ -515,8 +679,9 @@
 
 
 def finish_kernel(limits, spread_ref, pg_ref, energy_ref, obj_ref, probe_ref, illum_ref,
-                  onew_ref, pnew_ref, land_rows, land_cols, land_corners, total_ref, mate_half, mate_energy, warm, heat,
-                  box1, box2, box3, fold_send, fold_recv, mate_send, mate_recv, down_send, down_recv, up_send, up_recv,
+                  onew_ref, pnew_ref, land_rows, land_cols, land_inner, land_outer, out_cols, out_ends, passing, total_ref, mate_half, mate_energy, warm, heat,
+                  box1, box2, box3, seam_send, seam_recv, pass_send, pass_recv, near_send, near_recv, row_send, row_recv,
+                  corner_send, corner_recv, mate_send, mate_recv, down_send, down_recv, up_send, up_recv,
                   heat_send, heat_recv):
     cells = obj_ref.shape[1]
     row, col = place()
@@ -526,38 +691,96 @@
     units = len(ORDERS)
     unit = pg_ref.shape[1] // units
 
-    barrier, total = greet_sides(limits)
+    r = roles(limits)
+    barrier, total = greet(r)
     pl.semaphore_signal(barrier, inc=1, device_id=mate, device_id_type=MESH)
     for axis in range(3):
         for by in (1, 2, 3):
             pl.semaphore_signal(barrier, inc=1, device_id=along(axis, by), device_id_type=MESH)
     pl.semaphore_wait(barrier, total + 10)
 
-    def remote(src, dst, device, send, recv):
-        return pltpu.make_async_remote_copy(src_ref=src, dst_ref=dst, send_sem=send, recv_sem=recv,
-                                            device_id=device, device_id_type=MESH)
-
     firsts = [remote(energy_ref, mate_energy, mate, mate_send.at[0], mate_recv.at[0])]
     for u in range(units):
         rows = pl.ds(u * unit, unit)
         firsts.append(remote(pg_ref.at[1 - core, rows], mate_half.at[rows], mate, mate_send.at[1 + u], mate_recv.at[1 + u]))
+    half = cells // 2
+    seam, cols = r["seam"], r["cols"]
+    outer_from = pl.multiple_of(jnp.where(core == 0, 0, cells - HALO), HALO)
+    inner_from = pl.multiple_of(jnp.where(core == 0, cells - HALO, 0), HALO)
+    outer_at = pl.multiple_of(jnp.where(core == 0, 0, cells + HALO), HALO)
+    inner_at = pl.multiple_of(jnp.where(core == 0, cells + HALO, 0), HALO)
+    edge_from = {-1: 0, 1: cells - HALO}
+    rim_at = {-1: 0, 1: cells + HALO}
+    side = {-1: 0, 1: 1}
+    inside, nears, seams, ends, corners = {}, {}, {}, {}, {}
+
+    def region(top, tall, left, wide):
+        return spread_ref.at[:, pl.ds(top, tall), pl.ds(left, wide)]
+
+    for dc in (-1, 1):
+        i = side[dc]
+        inside[dc] = remote(region(inner_at, HALO, rim_at[dc], HALO), land_inner.at[i], mate, corner_send.at[i], corner_recv.at[i])
+        when(r["has"][dc], inside[dc].start)
     for copy in firsts:
         copy.start()
-
-    folds = []
-    for i, side in enumerate(SIDES):
-        here = present(side, limits)
-        back = SIDES.index((-side[0], -side[1]))
-        land = land_rows.at[back] if i < 2 else land_cols.at[back - 2] if i < 4 else land_corners.at[back - 4]
-        send = remote(spread_ref.at[:, rim(side[0], cells), rim(side[1], cells)], land, neighbour(side),
-                      fold_send.at[i], fold_recv.at[back])
-        mine = land_rows.at[i] if i < 2 else land_cols.at[i - 2] if i < 4 else land_corners.at[i - 4]
-        arrive = pltpu.make_async_copy(mine, mine, fold_recv.at[i])
-        folds.append((here, send, arrive, side, mine))
-
-        @pl.when(here)
-        def _(send=send):
-            send.start()
+    for dc in (-1, 1):
+        i = side[dc]
+
+        @pl.when(r["has"][dc])
+        def _(dc=dc, i=i):
+            inside[dc].wait_recv()
+            for part in range(2):
+                out_cols[i, part] = spread_ref[part, HALO:HALO + cells, rim_at[dc]:rim_at[dc] + HALO]
+                out_cols[i, part, pl.ds(inner_from, HALO), :] += land_inner[i, part]
+
+        seams[dc] = [remote(out_cols.at[i, :, pl.ds(part * half, half), :], passing.at[i], (row, target),
+                            seam_send.at[part], seam_recv.at[i]) for part, target in ((0, cols - 1), (1, 0))]
+        when(r["at_seam"][dc], seams[dc][0].start, seams[dc][1].start)
+
+    inner = remote(region(inner_at, HALO, HALO, cells), land_rows.at[1], mate, row_send.at[3], row_recv.at[3])
+    middle = remote(region(outer_at, HALO, 2 * HALO, cells - 2 * HALO), land_rows.at[0, :, :, pl.ds(HALO, cells - 2 * HALO)], r["outer"],
+                    row_send.at[2], row_recv.at[2])
+
+    def start_fold():
+        for dc in (-1, 1):
+            i = side[dc]
+            corners[dc] = (jnp.logical_and(r["has_outer"], r["has"][dc]),
+                           remote(region(outer_at, HALO, rim_at[dc], HALO), land_outer.at[1 - i], (row, col + dc),
+                                  corner_send.at[2 + i], corner_recv.at[3 - i]))
+            when(corners[dc][0], corners[dc][1].start)
+        when(r["has_outer"], middle.start)
+        for dc in (-1, 1):
+            i = side[dc]
+            nears[dc] = remote(out_cols.at[i], land_cols.at[1 - i], (row, col + dc), near_send.at[i], near_recv.at[1 - i])
+            when(r["near"][dc], nears[dc].start)
+        inner.start()
+
+    def forward(part, dc):
+        i = side[dc]
+        target = seam if dc == 1 else seam - 1
+        return remote(passing.at[i], land_cols.at[1 - i, :, pl.ds(part * half, half), :], (row, target), pass_send.at[i], pass_recv.at[part])
+
+    def relay(part, dc):
+        when(r["relay"][part], landed(passing.at[side[dc]], seam_recv.at[side[dc]]).wait, forward(part, dc).start)
+
+    def send_ends():
+        for dc in (-1, 1):
+            i = side[dc]
+            ends[dc] = remote(out_ends.at[i], land_rows.at[0, :, :, pl.ds(edge_from[dc], HALO)], r["outer"], row_send.at[i], row_recv.at[i])
+
+            @pl.when(r["has_outer"])
+            def _(dc=dc, i=i):
+                left = HALO + edge_from[dc]
+                for part in range(2):
+                    out_ends[i, part] = spread_ref[part, pl.ds(outer_at, HALO), left:left + HALO]
+
+                @pl.when(r["has"][dc])
+                def _():
+                    landed(land_outer.at[i], corner_recv.at[2 + i]).wait()
+                    for part in range(2):
+                        out_ends[i, part] += land_outer[i, part]
+
+                ends[dc].start()
 
     def piece(u, depth, spot):
         order = ORDERS[u]
@@ -606,6 +829,7 @@
         total_ref[rows, :] = pg_ref[core, rows, :] + mate_half[rows, :]
         flying.append(down(u, 1))
     waiting.extend(firsts)
+    start_fold()
 
     share = 1.0 / illum_ref[0]
     step_rows = 64
@@ -618,8 +842,15 @@
         return c
 
     lax.fori_loop(0, cells // step_rows, base, 0)
+    relay(0, -1)
+    relay(1, 1)
 
     for depth in (1, 2, 3):
+        if depth == 2:
+            send_ends()
+        if depth == 3:
+            relay(0, 1)
+            relay(1, -1)
         for copy in hot:
             copy.wait_recv()
         fresh = warm[depth - 1] + heat[depth - 1, 0] + heat[depth - 1, 1] + heat[depth - 1, 2]
@@ -668,13 +899,32 @@
                 got = pnew_ref.at[1 - core, rows]
                 lasts.append(pltpu.make_async_copy(got, got, mate_recv.at[5 + u]))
 
-    for here, send, arrive, side, mine in folds:
-        @pl.when(here)
-        def _(send=send, arrive=arrive, side=side, mine=mine):
-            send.wait_send()
-            arrive.wait()
+    inner.wait()
+    for part in range(2):
+        onew_ref[part, pl.ds(inner_from, HALO), :] += land_rows[1, part] * share
+
+    @pl.when(r["has_outer"])
+    def _():
+        middle.wait()
+        for dc in (-1, 1):
+            ends[dc].wait()
+        for part in range(2):
+            onew_ref[part, pl.ds(outer_from, HALO), :] += land_rows[0, part] * share
+
+    for dc in (-1, 1):
+        i = side[dc]
+        when(r["near"][dc], nears[dc].wait_send, landed(land_cols.at[i], near_recv.at[i]).wait)
+        when(r["at_seam"][dc], seams[dc][0].wait_send, seams[dc][1].wait_send)
+        for part in range(2):
+            when(r["at_seam"][dc], landed(land_cols.at[i, :, pl.ds(part * half, half), :], pass_recv.at[part]).wait)
+            when(r["relay"][part], forward(part, dc).wait_send)
+        when(corners[dc][0], corners[dc][1].wait_send)
+
+        @pl.when(r["has"][dc])
+        def _(dc=dc, i=i):
+            inside[dc].wait_send()
             for part in range(2):
-                onew_ref[part, edge(side[0], cells), edge(side[1], cells)] += mine[part] * share
+                onew_ref[part, :, edge_from[dc]:edge_from[dc] + HALO] += land_cols[i, part] * share
 
     for copy in lasts:
         copy.wait()
@@ -697,7 +947,11 @@
         scratch_shapes=[
             pltpu.VMEM((2, 2, HALO, cells), F32),
             pltpu.VMEM((2, 2, cells, HALO), F32),
-            pltpu.VMEM((4, 2, HALO, HALO), F32),
+            pltpu.VMEM((2, 2, HALO, HALO), F32),
+            pltpu.VMEM((2, 2, HALO, HALO), F32),
+            pltpu.VMEM((2, 2, cells, HALO), F32),
+            pltpu.VMEM((2, 2, HALO, HALO), F32),
+            pltpu.VMEM((2, 2, cells // 2, HALO), F32),
             pltpu.VMEM((rows, lanes), F32),
             pltpu.VMEM((rows, lanes), F32),
             pltpu.VMEM((8, 128), F32),
@@ -706,11 +960,12 @@
             pltpu.VMEM((units, 3, unit // 4, lanes), F32),
             pltpu.VMEM((units, 3, unit // 16, lanes), F32),
             pltpu.VMEM((units, 3, 8, 128), F32),
-            dma((8,)), dma((8,)), dma((9,)), dma((9,)),
+            dma((2,)), dma((2,)), dma((2,)), dma((2,)), dma((2,)), dma((2,)), dma((4,)), dma((4,)), dma((4,)), dma((4,)),
+            dma((9,)), dma((9,)),
             dma((units, 3, 3)), dma((units, 3, 3)), dma((units, 3, 3)), dma((units, 3, 3)),
             dma((3, 3)), dma((3, 3)),
         ],
-        compiler_params=pltpu.CompilerParams(collective_id=1, has_side_effects=True, vmem_limit_bytes=40 * 2**20),
+        compiler_params=pltpu.CompilerParams(collective_id=1, has_side_effects=True, vmem_limit_bytes=48 * 2**20),
     )(spread, pg, energy, obj, probe, illum)
 
 

time: 155 us -> 139 us (0.90)
  Pallas kernels: 141 us -> 127 us
  local copies, waits for them, and re-layouts: 12.5 us -> 10.9 us
    pallas_call x1, Pallas kernels: 74.2 us -> 59.9 us  [finish(): pl.pallas_call(functools.partial(finish_kernel, limits), out_shape=(jax.S...]
    unnamed x20 -> x14, local copies, waits for them, and re-layouts: 11 us -> 9.44 us
where the time goes in v4:
time: 139 us
  Pallas kernels  127 us (91%)
  local copies, waits for them, and re-layouts  10.9 us (8%)
    pallas_call x1, Pallas kernels, finish(): pl.pallas_call(functools.partial(finish_kernel, limits), out_shape=(jax.S...  59.9 us
    pallas_call x1, Pallas kernels, step(): pl.pallas_call(step_kernel, out_shape=(jax.ShapeDtypeStruct((2, rows, row...  44.6 us
    pallas_call x1, Pallas kernels, exchange_halo(): pl.pallas_call(functools.partial(halo_kernel, limits), out_shape=jax.Shap...  22.2 us
    unnamed x14, local copies, waits for them, and re-layouts  9.44 us

profile of v4, /device:TPU:1, one launch (start us, length us, event | category | flops | bytes accessed | tf_op | source)
XLA Modules:
  0.0 138.9 jit_solution(15781219933350906632)
XLA Ops:
  1.3 0.8 copy.10.pos_ref
  2.0 0.0 copy-start.1
  2.0 1.6 %copy-done.1 = f32[2,512,512]{2,1,0:T(8,128)S(1)} copy-done((f32[2,512,512]{2,1,0:T(8,128)S(1)}, f32[2,512,512]{2,1,0:T(8,128)}, u32[]{:S(2)}) %copy-start.1) | copy-done | bytes 2097176
  3.6 0.0 copy-start.3
  3.6 0.0 copy-start.4
  3.6 0.0 copy-start.5
  3.6 22.2 %shard_map.94.canvas_ref = f32[2,768,768]{2,1,0:T(8,128)S(1)} custom-call(f32[2,512,512]{2,1,0:T(8,128)S(1)} %copy-done.1), custom_call_target="tpu_custom_call" | custom-call | tf_op jit(solution)/shard_map/pallas_call | solution.py:648
  25.9 0.0 copy-start
  25.9 2.1 %copy-done = f32[2,768,768]{2,1,0:T(8,128)} copy-done((f32[2,768,768]{2,1,0:T(8,128)}, f32[2,768,768]{2,1,0:T(8,128)S(1)}, u32[]{:S(2)}) %copy-start) | copy-done | bytes 4718616
  28.0 0.0 copy-done.3
  28.0 0.0 copy-done.4
  28.0 0.0 copy-done.5
  28.0 44.6 %shard_map.95 = (f32[2,768,768]{2,1,0:T(8,128)}, f32[2,4,256,256]{3,2,1,0:T(8,128)}, f32[6,2]{1,0:T(8,128)S(1)}, f32[8,128]{1,0:T(8,128)S(1)}, f32[1]{0:T(128)}) custom-call(s32[6,2]{1,0:T(8,128)S(1)} %copy.10.pos_ref, s32[1]{0:T(128)} %bitcast.7.count_ref, f32[2,768,768]{2,1,0:T(8,128)} %copy-done, f32[2,4,256,256]{3,2,1,0:T(8,128)} %probe_ref.1, ...), custom_call_target="tpu_custom_call" | custom-call | tf_op jit(solution)/shard_map/pallas_call | solution.py:234
  72.6 59.9 %shard_map.96 = (f32[2,512,512]{2,1,0:T(8,128)S(1)}, f32[2,1024,256]{2,1,0:T(8,128)S(1)}) custom-call(f32[2,768,768]{2,1,0:T(8,128)} %get-tuple-element.10.spread_ref, f32[2,1024,256]{2,1,0:T(8,128)} %bitcast.11, f32[8,128]{1,0:T(8,128)S(1)} %get-tuple-element.12.energy_ref, f32[2,512,512]{2,1,0:T(8,128)} %obj_ref.3, f32[2,1024,256]{2,1,0:T(8,128)} %bitcast.10, ...), custom_call_target="tpu_custom_call" | custom-call | tf_op jit(solution)/shard_map/pallas_call | solution.py:942
  132.5 0.0 copy-start.2
  132.5 1.3 copy-done.2
  133.8 0.6 copy.11
  134.5 3.1 %copy.15 = f32[2,512,512]{2,1,0:T(8,128)} copy(f32[2,512,512]{2,1,0:T(8,128)} %copy-done.2) | data formatting | bytes 4194304
  137.6 1.3 copy.16
Async XLA Ops:
  2.0 1.6 %copy-start.1 = (f32[2,512,512]{2,1,0:T(8,128)S(1)}, f32[2,512,512]{2,1,0:T(8,128)}, u32[]{:S(2)}) copy-start(f32[2,512,512]{2,1,0:T(8,128)} %obj_ref.3) | copy-start | bytes 6291460
  3.6 24.4 %copy-start.3 = (f32[1,1,6,256,256]{4,3,2,1,0:T(8,128)S(1)}, f32[1,1,6,256,256]{4,3,2,1,0:T(8,128)}, u32[]{:S(2)}) copy-start(f32[1,1,6,256,256]{4,3,2,1,0:T(8,128)} %param.9) | copy-start | bytes 4718596
  3.6 24.4 %copy-start.4 = (bf16[4,2,256,256]{3,2,1,0:T(8,128)(2,1)S(1)}, bf16[4,2,256,256]{3,2,1,0:T(8,128)(2,1)}, u32[]{:S(2)}) copy-start(bf16[4,2,256,256]{3,2,1,0:T(8,128)(2,1)} %constant.4.clone.tab_ref) | copy-start | bytes 3145732
  3.6 24.4 %copy-start.5 = (bf16[256,256]{1,0:T(8,128)(2,1)S(1)}, bf16[256,256]{1,0:T(8,128)(2,1)}, u32[]{:S(2)}) copy-start(bf16[256,256]{1,0:T(8,128)(2,1)} %constant.5.clone.par_ref) | copy-start | bytes 393220
  25.9 2.1 %copy-start = (f32[2,768,768]{2,1,0:T(8,128)}, f32[2,768,768]{2,1,0:T(8,128)S(1)}, u32[]{:S(2)}) copy-start(f32[2,768,768]{2,1,0:T(8,128)S(1)} %shard_map.94.canvas_ref) | copy-start | bytes 14155780
  132.5 1.3 copy-start.2

commit v5 on v4

--- a/solution.py
+++ b/solution.py
@@ -251,7 +251,7 @@
             pltpu.VMEM((n, n // 2), F32),
             pltpu.VMEM((slots, 3, 8, 128), F32),
         ],
-        compiler_params=pltpu.CompilerParams(vmem_limit_bytes=50 * 2**20),
+        compiler_params=pltpu.CompilerParams(vmem_limit_bytes=60 * 2**20),
     )(pos, count, canvas, probe, amp, jnp.asarray(dft_tables(n)), jnp.asarray(parity_table(n)))
 
 
@@ -319,16 +319,19 @@
             action()
 
 
-def halo_kernel(limits, obj_ref, canvas_ref, zeros, passing, own_sem, zero_sems, row_send, row_recv, col_send, col_recv,
+def halo_kernel(limits, source_ref, canvas_ref, obj_ref, zeros, passing, load_sem, own_sem, zero_sems, row_send, row_recv, col_send, col_recv,
                 seam_send, seam_recv, pass_send, pass_recv, corner_send, corner_recv):
     cells = obj_ref.shape[1]
     half = cells // 2
+    load = pltpu.make_async_copy(source_ref, obj_ref, load_sem)
+    load.start()
     r = roles(limits)
     row, col, core, seam, cols = r["row"], r["col"], r["core"], r["seam"], r["cols"]
     barrier, total = greet(r)
     own = pltpu.make_async_copy(obj_ref, canvas_ref.at[:, pl.ds(HALO, cells), pl.ds(HALO, cells)], own_sem)
+    zeros[...] = jnp.zeros_like(zeros)
+    load.wait()
     own.start()
-    zeros[...] = jnp.zeros_like(zeros)
     pl.semaphore_wait(barrier, total)
 
     outer_from = pl.multiple_of(jnp.where(core == 0, 0, cells - HALO), HALO)
@@ -450,12 +453,13 @@
         in_specs=[pl.BlockSpec(memory_space=pl.ANY)],
         out_specs=pl.BlockSpec(memory_space=pl.ANY),
         scratch_shapes=[
+            pltpu.VMEM((2, cells, cells), F32),
             pltpu.VMEM((2, cells, cells + 2 * HALO), F32),
             pltpu.VMEM((2, 2, cells // 2, HALO), F32),
-            dma, dma((7,)), dma((4,)), dma((4,)), dma((2,)), dma((2,)), dma((2,)), dma((2,)), dma((2,)), dma((2,)),
+            dma, dma, dma((7,)), dma((4,)), dma((4,)), dma((2,)), dma((2,)), dma((2,)), dma((2,)), dma((2,)), dma((2,)),
             dma((4,)), dma((4,)),
         ],
-        compiler_params=pltpu.CompilerParams(collective_id=0, has_side_effects=True, vmem_limit_bytes=16 * 2**20),
+        compiler_params=pltpu.CompilerParams(collective_id=0, has_side_effects=True, vmem_limit_bytes=60 * 2**20),
     )(obj)
 
 
@@ -520,16 +524,19 @@
             action()
 
 
-def halo_kernel(limits, obj_ref, canvas_ref, zeros, passing, own_sem, zero_sems, row_send, row_recv, col_send, col_recv,
+def halo_kernel(limits, source_ref, canvas_ref, obj_ref, zeros, passing, load_sem, own_sem, zero_sems, row_send, row_recv, col_send, col_recv,
                 seam_send, seam_recv, pass_send, pass_recv, corner_send, corner_recv):
     cells = obj_ref.shape[1]
     half = cells // 2
+    load = pltpu.make_async_copy(source_ref, obj_ref, load_sem)
+    load.start()
     r = roles(limits)
     row, col, core, seam, cols = r["row"], r["col"], r["core"], r["seam"], r["cols"]
     barrier, total = greet(r)
     own = pltpu.make_async_copy(obj_ref, canvas_ref.at[:, pl.ds(HALO, cells), pl.ds(HALO, cells)], own_sem)
+    zeros[...] = jnp.zeros_like(zeros)
+    load.wait()
     own.start()
-    zeros[...] = jnp.zeros_like(zeros)
     pl.semaphore_wait(barrier, total)
 
     outer_from = pl.multiple_of(jnp.where(core == 0, 0, cells - HALO), HALO)
@@ -651,12 +658,13 @@
         in_specs=[pl.BlockSpec(memory_space=pl.ANY)],
         out_specs=pl.BlockSpec(memory_space=pl.ANY),
         scratch_shapes=[
+            pltpu.VMEM((2, cells, cells), F32),
             pltpu.VMEM((2, cells, cells + 2 * HALO), F32),
             pltpu.VMEM((2, 2, cells // 2, HALO), F32),
-            dma, dma((7,)), dma((4,)), dma((4,)), dma((2,)), dma((2,)), dma((2,)), dma((2,)), dma((2,)), dma((2,)),
+            dma, dma, dma((7,)), dma((4,)), dma((4,)), dma((2,)), dma((2,)), dma((2,)), dma((2,)), dma((2,)), dma((2,)),
             dma((4,)), dma((4,)),
         ],
-        compiler_params=pltpu.CompilerParams(collective_id=0, has_side_effects=True, vmem_limit_bytes=16 * 2**20),
+        compiler_params=pltpu.CompilerParams(collective_id=0, has_side_effects=True, vmem_limit_bytes=60 * 2**20),
     )(obj)
 
 
@@ -965,7 +973,7 @@
             dma((units, 3, 3)), dma((units, 3, 3)), dma((units, 3, 3)), dma((units, 3, 3)),
             dma((3, 3)), dma((3, 3)),
         ],
-        compiler_params=pltpu.CompilerParams(collective_id=1, has_side_effects=True, vmem_limit_bytes=48 * 2**20),
+        compiler_params=pltpu.CompilerParams(collective_id=1, has_side_effects=True, vmem_limit_bytes=60 * 2**20),
     )(spread, pg, energy, obj, probe, illum)
 
 

time: 139 us -> 138 us (level)
  local copies, waits for them, and re-layouts: 10.9 us -> 6.56 us
  Pallas kernels: 127 us -> 129 us
    pallas_call x1, Pallas kernels: 59.9 us -> 74.3 us  [finish(): pl.pallas_call(functools.partial(finish_kernel, limits), out_shape=(jax.S...]
    pallas_call x1, Pallas kernels: 44.6 us -> 32.6 us  [step(): pl.pallas_call(step_kernel, out_shape=(jax.ShapeDtypeStruct((2, rows, row...]
    unnamed x14 -> x6, local copies, waits for them, and re-layouts: 9.44 us -> 4.56 us
where the time goes in v5:
time: 138 us; the launch traced here: 137 us
  Pallas kernels  129 us (93%)
  local copies, waits for them, and re-layouts  6.56 us (5%)
    pallas_call x1, Pallas kernels, finish(): pl.pallas_call(functools.partial(finish_kernel, limits), out_shape=(jax.S...  74.3 us
    pallas_call x1, Pallas kernels, step(): pl.pallas_call(step_kernel, out_shape=(jax.ShapeDtypeStruct((2, rows, row...  32.6 us
    pallas_call x1, Pallas kernels, exchange_halo(): pl.pallas_call(functools.partial(halo_kernel, limits), out_shape=jax.Shap...  22.3 us
    unnamed x6, local copies, waits for them, and re-layouts  4.56 us

profile of v5, /device:TPU:1, one launch (start us, length us, event | category | flops | bytes accessed | tf_op | source)
XLA Modules:
  0.0 137.0 jit_solution(11674590503488637570)
XLA Ops:
  1.3 1.4 copy.10.pos_ref
  2.6 22.3 %shard_map.94.canvas_ref = f32[2,768,768]{2,1,0:T(8,128)} custom-call(f32[2,512,512]{2,1,0:T(8,128)} %obj_ref.1), custom_call_target="tpu_custom_call" | custom-call | tf_op jit(solution)/shard_map/pallas_call | solution.py:655
  24.9 32.6 %shard_map.95 = (f32[2,768,768]{2,1,0:T(8,128)}, f32[2,4,256,256]{3,2,1,0:T(8,128)}, f32[6,2]{1,0:T(8,128)}, f32[8,128]{1,0:T(8,128)}, f32[1]{0:T(128)}) custom-call(s32[6,2]{1,0:T(8,128)} %copy.10.pos_ref, s32[1]{0:T(128)} %bitcast.7.count_ref, f32[2,768,768]{2,1,0:T(8,128)} %shard_map.94.canvas_ref, f32[2,4,256,256]{3,2,1,0:T(8,128)} %probe_ref.1, ...), custom_call_target="tpu_custom_call" | custom-call | tf_op jit(solution)/shard_map/pallas_call | solution.py:234
  57.5 0.0 copy-start.1
  57.5 74.3 %shard_map.96 = (f32[2,512,512]{2,1,0:T(8,128)}, f32[2,1024,256]{2,1,0:T(8,128)}) custom-call(f32[2,768,768]{2,1,0:T(8,128)} %get-tuple-element.10.spread_ref, f32[2,1024,256]{2,1,0:T(8,128)} %bitcast.9, f32[8,128]{1,0:T(8,128)} %get-tuple-element.12.energy_ref, f32[2,512,512]{2,1,0:T(8,128)} %obj_ref.1, f32[2,1024,256]{2,1,0:T(8,128)} %bitcast.8, ...), custom_call_target="tpu_custom_call" | custom-call | tf_op jit(solution)/shard_map/pallas_call | solution.py:950
  131.8 0.0 copy-done.1
  131.8 0.6 copy.11
  132.5 0.0 copy-start
  132.5 3.2 %copy.15 = f32[2,512,512]{2,1,0:T(8,128)} copy(f32[2,512,512]{2,1,0:T(8,128)} %get-tuple-element.20) | data formatting | bytes 4194304
  135.7 0.0 copy-done
  135.7 1.3 copy.16
Async XLA Ops:
  57.5 74.3 %copy-start.1 = (f32[6,2]{1,0:T(8,128)S(1)}, f32[6,2]{1,0:T(8,128)}, u32[]{:S(2)}) copy-start(f32[6,2]{1,0:T(8,128)} %get-tuple-element.16) | copy-start | bytes 148
  132.5 3.2 %copy-start = (f32[2,1024,256]{2,1,0:T(8,128)S(1)}, f32[2,1024,256]{2,1,0:T(8,128)}, u32[]{:S(2)}) copy-start(f32[2,1024,256]{2,1,0:T(8,128)} %get-tuple-element.15) | copy-start | bytes 6291460

commit v6 on v5

--- a/solution.py
+++ b/solution.py
@@ -134,9 +134,9 @@
     return down, across
 
 
-def step_kernel(pos_ref, count_ref, canvas_ref, probe_ref, amp_ref, tab_ref, par_ref,
+def step_kernel(pos_ref, count_ref, canvas_ref, probe_ref, amp_ref, tab_ref,
                 spread_ref, pg_ref, shift_ref, energy_ref, illum_ref,
-                patch, far, inten, grad, col0, col1, sums):
+                patch, far, inten, grad, sums):
     n = probe_ref.shape[2]
     h = n // 2
     modes = probe_ref.shape[1]
@@ -179,12 +179,7 @@
             return c
 
         lax.fori_loop(0, modes, forward, 0, unroll=UNROLL)
-        hi, lo = split(amp_ref[s])
-        am = mm(hi, par_ref[...]) + mm(lo, par_ref[...])
-        col0[...] = am[:, :h]
-        col1[...] = am[:, h:]
-        am = jnp.concatenate([jnp.concatenate([col[pl.ds(p, h, 2), :] for p in range(2)], 0) for col in (col0, col1)], 1)
-        inten[...] = am * lax.rsqrt(jnp.maximum(inten[...], INTENSITY_FLOOR)) - 1.0
+        inten[...] = amp_ref[s] * lax.rsqrt(jnp.maximum(inten[...], INTENSITY_FLOOR)) - 1.0
         grad[...] = jnp.zeros_like(grad)
 
         def backward(k, c):
@@ -240,19 +235,17 @@
             jax.ShapeDtypeStruct((8, 128), F32),
             jax.ShapeDtypeStruct((1,), F32),
         ),
-        in_specs=[smem, smem, vmem, vmem, vmem, vmem, vmem],
+        in_specs=[smem, smem, vmem, vmem, vmem, vmem],
         out_specs=(vmem, vmem, smem, vmem, smem),
         scratch_shapes=[
             pltpu.VMEM((2, n, n), F32),
             pltpu.VMEM((modes, 2, n, n), F32),
             pltpu.VMEM((n, n), F32),
             pltpu.VMEM((2, n, n), F32),
-            pltpu.VMEM((n, n // 2), F32),
-            pltpu.VMEM((n, n // 2), F32),
             pltpu.VMEM((slots, 3, 8, 128), F32),
         ],
         compiler_params=pltpu.CompilerParams(vmem_limit_bytes=60 * 2**20),
-    )(pos, count, canvas, probe, amp, jnp.asarray(dft_tables(n)), jnp.asarray(parity_table(n)))
+    )(pos, count, canvas, probe, amp, jnp.asarray(dft_tables(n)))
 
 
 MESH = pl.DeviceIdType.MESH
@@ -524,12 +517,15 @@
             action()
 
 
-def halo_kernel(limits, source_ref, canvas_ref, obj_ref, zeros, passing, load_sem, own_sem, zero_sems, row_send, row_recv, col_send, col_recv,
+def halo_kernel(limits, source_ref, amp_ref, par_ref, flip_ref, canvas_ref, order_ref, obj_ref, amp, zeros, passing,
+                amp_sem, load_sem, own_sem, zero_sems, row_send, row_recv, col_send, col_recv,
                 seam_send, seam_recv, pass_send, pass_recv, corner_send, corner_recv):
     cells = obj_ref.shape[1]
     half = cells // 2
     load = pltpu.make_async_copy(source_ref, obj_ref, load_sem)
     load.start()
+    take = pltpu.make_async_copy(amp_ref, amp, amp_sem)
+    take.start()
     r = roles(limits)
     row, col, core, seam, cols = r["row"], r["col"], r["core"], r["seam"], r["cols"]
     barrier, total = greet(r)
@@ -617,6 +613,17 @@
         when(give, corners[dc][1].start)
     relay(0, 1)
     relay(1, -1)
+    take.wait()
+
+    def sort(s, c):
+        hi, lo = split(amp[s])
+        hi, lo = split(mm(hi, par_ref[...]) + mm(lo, par_ref[...]))
+        amp[s] = mm(flip_ref[...], hi) + mm(flip_ref[...], lo)
+        return c
+
+    lax.fori_loop(0, amp.shape[0], sort, 0)
+    give_back = pltpu.make_async_copy(amp, order_ref, amp_sem)
+    give_back.start()
     inside = {}
     for dc in (-1, 1):
         i = side[dc]
@@ -643,29 +650,34 @@
     for cond, copy in blanks:
         when(cond, copy.wait)
     own.wait()
+    give_back.wait()
 
 
 def outer_at_of_mate(at, cells):
     return pl.multiple_of(cells + HALO - at, HALO)
 
 
-def exchange_halo(obj, limits):
+def exchange_halo(obj, amp, limits):
+    n = amp.shape[1]
+    par = parity_table(n)
+    vmem = pl.BlockSpec(memory_space=pltpu.VMEM)
     cells = obj.shape[1]
     dma = pltpu.SemaphoreType.DMA
     return pl.pallas_call(
         functools.partial(halo_kernel, limits),
-        out_shape=jax.ShapeDtypeStruct((2, cells + 2 * HALO, cells + 2 * HALO), F32),
-        in_specs=[pl.BlockSpec(memory_space=pl.ANY)],
-        out_specs=pl.BlockSpec(memory_space=pl.ANY),
+        out_shape=(jax.ShapeDtypeStruct((2, cells + 2 * HALO, cells + 2 * HALO), F32), jax.ShapeDtypeStruct(amp.shape, F32)),
+        in_specs=[pl.BlockSpec(memory_space=pl.ANY), pl.BlockSpec(memory_space=pl.ANY), vmem, vmem],
+        out_specs=(pl.BlockSpec(memory_space=pl.ANY), pl.BlockSpec(memory_space=pl.ANY)),
         scratch_shapes=[
             pltpu.VMEM((2, cells, cells), F32),
+            pltpu.VMEM(amp.shape, F32),
             pltpu.VMEM((2, cells, cells + 2 * HALO), F32),
             pltpu.VMEM((2, 2, cells // 2, HALO), F32),
-            dma, dma, dma((7,)), dma((4,)), dma((4,)), dma((2,)), dma((2,)), dma((2,)), dma((2,)), dma((2,)), dma((2,)),
+            dma, dma, dma, dma((7,)), dma((4,)), dma((4,)), dma((2,)), dma((2,)), dma((2,)), dma((2,)), dma((2,)), dma((2,)),
             dma((4,)), dma((4,)),
         ],
         compiler_params=pltpu.CompilerParams(collective_id=0, has_side_effects=True, vmem_limit_bytes=60 * 2**20),
-    )(obj)
+    )(obj, amp, jnp.asarray(par), jnp.asarray(np.ascontiguousarray(par.T)))
 
 
 SIDES = [(-1, 0), (1, 0), (0, -1), (0, 1), (-1, -1), (-1, 1), (1, -1), (1, 1)]
@@ -978,8 +990,8 @@
 
 
 def body(limits, object_field, probe, amplitudes, positions, counts):
-    canvas = exchange_halo(object_field, limits)
-    spread, probe_grad, shift, energy, illum = step(positions[0, 0], counts[0], canvas, probe, amplitudes[0, 0])
+    canvas, order = exchange_halo(object_field, amplitudes[0, 0], limits)
+    spread, probe_grad, shift, energy, illum = step(positions[0, 0], counts[0], canvas, probe, order)
     n = probe.shape[2]
     flat = (2, probe.shape[1] * n, n)
     object_new, probe_new = finish(spread, probe_grad.reshape(flat), energy, object_field, probe.reshape(flat), illum, limits)

time: 138 us -> 137 us (level)
    pallas_call x1, Pallas kernels: 74.3 us -> 68.4 us  [finish(): pl.pallas_call(functools.partial(finish_kernel, limits), out_shape=(jax.S...]
    pallas_call x1, Pallas kernels: 32.6 us -> 37.8 us  [step(): pl.pallas_call(step_kernel, out_shape=(jax.ShapeDtypeStruct((2, rows, row...]
where the time goes in v6:
time: 137 us
  Pallas kernels  129 us (94%)
  local copies, waits for them, and re-layouts  6.56 us (5%)
    pallas_call x1, Pallas kernels, finish(): pl.pallas_call(functools.partial(finish_kernel, limits), out_shape=(jax.S...  68.4 us
    pallas_call x1, Pallas kernels, step(): pl.pallas_call(step_kernel, out_shape=(jax.ShapeDtypeStruct((2, rows, row...  37.8 us
    pallas_call x1, Pallas kernels, exchange_halo(): pl.pallas_call(functools.partial(halo_kernel, limits), out_shape=(jax.Sha...  23.2 us
    unnamed x6, local copies, waits for them, and re-layouts  4.56 us

profile of v6, /device:TPU:1, one launch (start us, length us, event | category | flops | bytes accessed | tf_op | source)
XLA Modules:
  0.0 137.3 jit_solution(17793120053857863127)
XLA Ops:
  1.3 1.4 copy.11.pos_ref
  2.6 23.2 %shard_map.103 = (f32[2,768,768]{2,1,0:T(8,128)}, f32[6,256,256]{2,1,0:T(8,128)}) custom-call(f32[2,512,512]{2,1,0:T(8,128)} %obj_ref.1, f32[6,256,256]{2,1,0:T(8,128)} %bitcast.11, bf16[256,256]{1,0:T(8,128)(2,1)} %constant.6.clone.par_ref, bf16[256,256]{1,0:T(8,128)(2,1)} %constant.7.clone.flip_ref), custom_call_target="tpu_custom_call" | custom-call | tf_op jit(solution)/shard_map/pallas_call | solution.py:666
  25.9 37.8 %shard_map.104 = (f32[2,768,768]{2,1,0:T(8,128)}, f32[2,4,256,256]{3,2,1,0:T(8,128)}, f32[6,2]{1,0:T(8,128)}, f32[8,128]{1,0:T(8,128)}, f32[1]{0:T(128)}) custom-call(s32[6,2]{1,0:T(8,128)} %copy.11.pos_ref, s32[1]{0:T(128)} %bitcast.7.count_ref, f32[2,768,768]{2,1,0:T(8,128)} %get-tuple-element.12.canvas_ref, f32[2,4,256,256]{3,2,1,0:T(8,128)} %probe_ref.1, ...), custom_call_target="tpu_custom_call" | custom-call | tf_op jit(solution)/shard_map/pallas_call | solution.py:229
  63.7 0.0 copy-start.1
  63.7 68.4 %shard_map.105 = (f32[2,512,512]{2,1,0:T(8,128)}, f32[2,1024,256]{2,1,0:T(8,128)}) custom-call(f32[2,768,768]{2,1,0:T(8,128)} %get-tuple-element.14.spread_ref, f32[2,1024,256]{2,1,0:T(8,128)} %bitcast.9, f32[8,128]{1,0:T(8,128)} %get-tuple-element.16.energy_ref, f32[2,512,512]{2,1,0:T(8,128)} %obj_ref.1, f32[2,1024,256]{2,1,0:T(8,128)} %bitcast.8, ...), custom_call_target="tpu_custom_call" | custom-call | tf_op jit(solution)/shard_map/pallas_call | solution.py:962
  132.1 0.0 copy-done.1
  132.1 0.6 copy.12
  132.8 0.0 copy-start
  132.8 3.2 %copy.16 = f32[2,512,512]{2,1,0:T(8,128)} copy(f32[2,512,512]{2,1,0:T(8,128)} %get-tuple-element.24) | data formatting | bytes 4194304
  136.0 0.0 copy-done
  136.0 1.3 copy.17
Async XLA Ops:
  63.7 68.4 %copy-start.1 = (f32[6,2]{1,0:T(8,128)S(1)}, f32[6,2]{1,0:T(8,128)}, u32[]{:S(2)}) copy-start(f32[6,2]{1,0:T(8,128)} %get-tuple-element.20) | copy-start | bytes 148
  132.8 3.2 %copy-start = (f32[2,1024,256]{2,1,0:T(8,128)S(1)}, f32[2,1024,256]{2,1,0:T(8,128)}, u32[]{:S(2)}) copy-start(f32[2,1024,256]{2,1,0:T(8,128)} %get-tuple-element.19) | copy-start | bytes 6291460
